TPU v7x, 256 devices: a whole 4x4x8 slice. The times are simulated.
256 devices in a mesh: lat: 32 (over x, y, core), depth: 8 (over z).
Axes of the slice: x: 4, y: 4, z: 8, core: 2. Of those that a mesh axis runs over, the one named last changes fastest.
Arguments:
- own_basis: bfloat16 [32, 1280, 64, 128], P(None, 'lat', 'depth'), may hold values from -1 to 1
- left_margin: bfloat16 [32, 512, 64, 128], P(None, 'lat', 'depth'), may hold values from -1 to 1
- right_margin: bfloat16 [32, 512, 64, 128], P(None, 'lat', 'depth'), may hold values from -1 to 1
- permeability: float32 [1280, 64, 128], P('lat', 'depth'), may hold values from 0 to 21, as said below
- cluster_mask: int32 [1280, 64], P('lat', 'depth'), may hold values 0 or 1
- intersection_width: int32 [32, 8, 2], P('lat', 'depth'), may hold values from 0 to 16, as said below
Outputs:
- lateral_rows: float32 [32, 8, 3, 32, 32], P('lat', 'depth')
- vertical_rows: float32 [32, 8, 2, 3, 32, 32], P('lat', 'depth')
Inputs may be any that keep to these rules, and one draw needn't show every extreme that they name: `intersection_width`: A subdomain's reach in east cells into its left (last index 0) and right (last index 1) neighbour: a multiple of 8, 0 exactly where that neighbour lies outside the grid, 8 or more otherwise, and 16 for at least one subdomain. `permeability`: Positive.
All inputs are finite; a program needn't handle non-finite values. No bound on the sum of `cluster_mask` on one device may be relied on, other than what follows from the above.
Results may differ from a plain program's by a relative error of at most 0.00036.
Values may be sent and summed in bfloat16 or wider, within the bound.
A program may use at most 128 MiB of HBM per device.

v0:
```python
import jax
import jax.numpy as jnp
from jax import lax
from jax.sharding import PartitionSpec as P

diagonal_weight = 6.1


def shifted(value, axis, steps):
    count = lax.axis_size(axis)
    initial, last = (max(0, -steps), min(count, count - steps))
    return lax.ppermute(value, axis, [(source, source + steps) for source in range(initial, last)])


def scaled(factor, values):
    return (factor.astype(jnp.float32) * values.astype(jnp.float32)).astype(jnp.bfloat16)


def pair_gram(left_part, right_part):
    left_flat = left_part.reshape(left_part.shape[0], -1)
    right_flat = right_part.reshape(right_part.shape[0], -1)
    return lax.dot_general(
        left_flat, right_flat, (((1,), (1,)), ((), ())), preferred_element_type=jnp.float32
    )


def energy(field_planes):
    inner_cells = field_planes[:, 1:-1]
    energy_sum = diagonal_weight * pair_gram(inner_cells, inner_cells)
    energy_sum = (
        energy_sum
        - pair_gram(inner_cells, field_planes[:, 2:])
        - pair_gram(inner_cells, field_planes[:, :-2])
    )
    north_pairs = pair_gram(inner_cells[:, :, :, :-1], inner_cells[:, :, :, 1:])
    depth_pairs = pair_gram(inner_cells[:, :, :-1], inner_cells[:, :, 1:])
    return energy_sum - north_pairs - north_pairs.T - depth_pairs - depth_pairs.T


def keep_margins(left_part, right_part, widths):
    plane_index = jnp.arange(left_part.shape[1], dtype=jnp.int32)[None, :, None, None]
    kept_left = jnp.where(
        plane_index >= left_part.shape[1] - widths[0], left_part, jnp.zeros_like(left_part)
    )
    kept_right = jnp.where(plane_index < widths[1], right_part, jnp.zeros_like(right_part))
    return (kept_left, kept_right)


def build_fields(own_field, kept_left, kept_right, scaling, from_west, from_east):
    west_strip, west_edge, west_scaling = from_west
    east_strip, east_edge, east_scaling = from_east
    east_cells = own_field.shape[1]
    margin = kept_left.shape[1]
    own_west = scaled(west_scaling[None], kept_left[:, margin - 1 :])
    own_east = scaled(east_scaling[None], kept_right[:, :1])
    left_field = scaled(scaling[None, :margin], west_strip)
    right_field = scaled(scaling[None, east_cells - margin :], east_strip)
    return (own_field, own_west, own_east, left_field, west_edge, right_field, east_edge)


def lateral_blocks(pieces):
    own_field, own_west, own_east, left_field, west_edge, right_field, east_edge = pieces
    basis_count = own_field.shape[0]
    east_cells = own_field.shape[1]
    margin = left_field.shape[1]
    blank_planes = jnp.zeros((basis_count, 2) + own_field.shape[2:], jnp.bfloat16)
    whole_block = energy(jnp.concatenate([own_west, own_field, own_east], 1))
    west_self = jnp.concatenate([own_west, own_field[:, : margin + 2]], 1)
    west_other = jnp.concatenate([west_edge, left_field, blank_planes], 1)
    west_block = energy(jnp.concatenate([west_self, west_other], 0))
    east_self = jnp.concatenate([own_field[:, east_cells - margin - 2 :], own_east], 1)
    east_other = jnp.concatenate([blank_planes, right_field, east_edge], 1)
    east_block = energy(jnp.concatenate([east_self, east_other], 0))
    zero_block = jnp.zeros((basis_count, basis_count), jnp.float32)
    first_row = jnp.stack(
        [
            whole_block,
            west_block[:basis_count, basis_count:],
            east_block[:basis_count, basis_count:],
        ]
    )
    second_row = jnp.stack(
        [west_block[basis_count:, :basis_count], west_block[basis_count:, basis_count:], zero_block]
    )
    third_row = jnp.stack(
        [east_block[basis_count:, :basis_count], zero_block, east_block[basis_count:, basis_count:]]
    )
    return jnp.stack([first_row, second_row, third_row])


def depth_plane(pieces, plane_at):
    own_field, own_west, own_east, left_field, west_edge, right_field, east_edge = pieces
    basis_count = own_field.shape[0]
    east_cells = own_field.shape[1]
    margin = left_field.shape[1]
    gap_zeros = jnp.zeros((basis_count, east_cells - margin, own_field.shape[3]), jnp.bfloat16)
    left_plane = jnp.concatenate([left_field[:, :, plane_at], gap_zeros], 1)
    right_plane = jnp.concatenate([gap_zeros, right_field[:, :, plane_at]], 1)
    return jnp.concatenate([own_field[:, :, plane_at], left_plane, right_plane], 0)


def to_blocks(matrix, basis_count):
    return matrix.reshape(3, basis_count, 3, basis_count).transpose(0, 2, 1, 3)


def assemble(own_rows, west_rows, east_rows):
    left_block = own_rows[..., 1, :, :] + west_rows[..., 0, :, :]
    middle_block = own_rows[..., 0, :, :] + west_rows[..., 2, :, :] + east_rows[..., 1, :, :]
    right_block = own_rows[..., 2, :, :] + east_rows[..., 0, :, :]
    return jnp.stack([left_block, middle_block, right_block], -3)


def body(own_basis, left_margin, right_margin, permeability, cluster_mask, intersection_width):
    basis_count = own_basis.shape[0]
    east_cells = own_basis.shape[1]
    layers = own_basis.shape[2]
    scaling = jnp.sqrt(
        permeability * (0.05 + 0.95 * cluster_mask.astype(jnp.float32))[:, :, None]
    ).astype(jnp.bfloat16)
    kept_left, kept_right = keep_margins(left_margin, right_margin, intersection_width[0, 0])
    own_field = scaled(scaling[None], own_basis)
    from_west = shifted(
        (kept_right, own_field[:, east_cells - 1 :], scaling[east_cells - 1 :]), "lat", 1
    )
    from_east = shifted((kept_left, own_field[:, :1], scaling[:1]), "lat", -1)
    pieces = build_fields(own_field, kept_left, kept_right, scaling, from_west, from_east)
    bottom_plane = depth_plane(pieces, 0)
    top_plane = depth_plane(pieces, layers - 1)
    below_top = shifted(top_plane, "depth", 1)
    lateral = lateral_blocks(pieces)
    down_pairs = -pair_gram(bottom_plane, below_top)
    above_bottom = shifted(bottom_plane, "depth", -1)
    up_pairs = -pair_gram(top_plane, above_bottom)
    blocks = jnp.stack(
        [lateral, to_blocks(down_pairs, basis_count), to_blocks(up_pairs, basis_count)]
    )
    west_rows = shifted(blocks[:, 2], "lat", 1)
    east_rows = shifted(blocks[:, 1], "lat", -1)
    row_blocks = assemble(blocks[:, 0], west_rows, east_rows)
    return (row_blocks[0][None, None], row_blocks[1:][None, None])


def solution(mesh):
    in_specs = (
        P(None, "lat", "depth", None),
        P(None, "lat", "depth", None),
        P(None, "lat", "depth", None),
        P("lat", "depth", None),
        P("lat", "depth"),
        P("lat", "depth", None),
    )
    out_specs = (P("lat", "depth", None, None, None), P("lat", "depth", None, None, None, None))
    return jax.shard_map(body, mesh=mesh, in_specs=in_specs, out_specs=out_specs, check_vma=False)
```

profile of v0, /device:TPU:153, one launch (start us, length us, event | category | flops | bytes accessed | tf_op | source)
XLA Modules:
  0.0 115.0 jit_solution(4933149447915775426)
XLA Ops:
  0.6 0.8 multiply_add_fusion
  1.5 1.0 sqrt_convert_fusion
  2.5 0.6 fusion.173
  3.1 3.3 %collective-permute-start.1 = (bf16[1,8,128]{2,1,0:T(8,128)(2,1)}, bf16[1,8,128]{2,1,0:T(8,128)(2,1)}, u32[]{:S(2)}, u32[]{:S(2)}) collective-permute-start(bf16[1,8,128]{2,1,0:T(8,128)(2,1)} %get-tuple-element.36), channel_id=1, source_target_pairs={{0,8},{8,16},{16,24},{24,32},{32,40},{40,48},{48,56},{56,64},{64,7... | collective-permute-start | bytes 6152 | tf_op jit(solution)/shard_map/ppermute | solution.py:12
  6.5 2.2 %collective-permute-start = (bf16[1,8,128]{2,1,0:T(8,128)(2,1)}, bf16[1,8,128]{2,1,0:T(8,128)(2,1)}, u32[]{:S(2)}, u32[]{:S(2)}) collective-permute-start(bf16[1,8,128]{2,1,0:T(8,128)(2,1)} %get-tuple-element.37), channel_id=1, source_target_pairs={{8,0},{16,8},{24,16},{32,24},{40,32},{48,40},{56,48},{64,56},{72,6... | collective-permute-start | bytes 6152 | tf_op jit(solution)/shard_map/ppermute | solution.py:12
  8.7 1.3 %fusion.174 = (s32[1,1,1]{2,1,0:T(1,128)}, s32[1,1,1]{2,1,0:T(1,128)}) fusion(s32[1,1,2]{2,1,0:T(1,128)} %param.11), kind=kLoop, calls=%fused_computation.154 | loop fusion | bytes 16 | tf_op jit(solution)/shard_map/slice | solution.py:45
  10.7 3.4 %copy_select_fusion = bf16[32,16,8,128]{3,0,1,2:T(8,128)(2,1)} fusion(bf16[32,16,8,128]{3,2,1,0:T(8,128)(2,1)} %param.7, pred[16]{0:T(512)(128)(4,1)S(1)} %iota_compare_fusion.3), kind=kLoop, calls=%fused_computation.94 | loop fusion | flops 524288 | bytes 2097168 | tf_op jit(solution)/shard_map/jit(_where)/select_n | solution.py:42
  14.1 2.9 %collective-permute-start.4 = (bf16[32,16,8,128]{3,0,1,2:T(8,128)(2,1)}, bf16[32,16,8,128]{3,0,1,2:T(8,128)(2,1)}, u32[]{:S(2)}, u32[]{:S(2)}) collective-permute-start(bf16[32,16,8,128]{3,0,1,2:T(8,128)(2,1)} %copy_select_fusion), channel_id=1, source_target_pairs={{8,0},{16,8},{24,16},{32,24},{40,32},{48,40},{56,48},{64,56},{72,6... | collective-permute-start | bytes 3145736 | tf_op jit(solution)/shard_map/ppermute | solution.py:12
  17.0 0.7 iota_compare_fusion.4
  17.6 1.7 %copy_select_fusion.1 = bf16[32,16,8,128]{3,0,2,1:T(8,128)(2,1)} fusion(bf16[32,16,8,128]{3,2,1,0:T(8,128)(2,1)S(1)} %copy-done.9, pred[16]{0:T(512)(128)(4,1)S(1)} %iota_compare_fusion.4), kind=kLoop, calls=%fused_computation.95 | loop fusion | flops 524288 | bytes 2097168 | tf_op jit(solution)/shard_map/jit(_where)/select_n | solution.py:45
  19.3 4.8 %collective-permute-start.3 = (bf16[32,16,8,128]{3,0,2,1:T(8,128)(2,1)}, bf16[32,16,8,128]{3,0,2,1:T(8,128)(2,1)}, u32[]{:S(2)}, u32[]{:S(2)}) collective-permute-start(bf16[32,16,8,128]{3,0,2,1:T(8,128)(2,1)} %copy_select_fusion.1), channel_id=1, source_target_pairs={{0,8},{8,16},{16,24},{24,32},{32,40},{40,48},{48,56},{56,64},{64,7... | collective-permute-start | bytes 3145736 | tf_op jit(solution)/shard_map/ppermute | solution.py:12
  24.2 1.9 %multiply_convert_fusion = bf16[32,40,8,128]{3,0,1,2:T(8,128)(2,1)S(1)} fusion(bf16[32,40,8,128]{3,2,1,0:T(8,128)(2,1)S(1)} %copy-done.2, f32[40,8,128]{2,0,1:T(8,128)S(1)} %copy.57), kind=kLoop, calls=%fused_computation | loop fusion | flops 3932160 | bytes 5406720 | tf_op jit(solution)/shard_map/convert_element_type | solution.py:16
  26.1 0.6 fusion.166
  26.7 2.4 %collective-permute-start.2 = (bf16[32,1,8,128]{3,0,1,2:T(8,128)(2,1)}, bf16[32,1,8,128]{3,0,1,2:T(8,128)(2,1)S(1)}, u32[]{:S(2)}, u32[]{:S(2)}) collective-permute-start(bf16[32,1,8,128]{3,0,1,2:T(8,128)(2,1)} %get-tuple-element.8), channel_id=1, source_target_pairs={{0,8},{8,16},{16,24},{24,32},{32,40},{40,48},{48,56},{56,64},{64,7... | collective-permute-start | bytes 196616 | tf_op jit(solution)/shard_map/ppermute | solution.py:12
  29.2 1.9 %fusion.165 = (bf16[32,18,8,128]{3,0,1,2:T(8,128)(2,1)}, bf16[32,18,8,128]{3,0,1,2:T(8,128)(2,1)}) fusion(bf16[32,40,8,128]{3,0,1,2:T(8,128)(2,1)S(1)} %multiply_convert_fusion), kind=kLoop, calls=%fused_computation.145 | loop fusion | bytes 4718592 | tf_op jit(solution)/shard_map/slice | solution.py:68
  31.1 0.9 fusion.164
  32.1 1.2 %fusion.163 = (bf16[32,40,8,127]{3,0,1,2:T(8,128)(2,1)S(1)}, bf16[32,40,8,127]{3,0,1,2:T(8,128)(2,1)S(1)}) fusion(bf16[32,40,8,128]{3,0,1,2:T(8,128)(2,1)S(1)} %multiply_convert_fusion), kind=kLoop, calls=%fused_computation.143 | loop fusion | bytes 10403840 | tf_op jit(solution)/shard_map/slice | solution.py:35
  33.2 0.7 fusion.149
  34.0 1.5 %fusion.136 = f32[32,32]{1,0:T(8,128)} fusion(bf16[32,40,8,127]{3,0,1,2:T(8,128)(2,1)S(1)} %get-tuple-element.3, bf16[32,40,8,127]{3,0,1,2:T(8,128)(2,1)S(1)} %get-tuple-element.2), kind=kOutput, calls=%fused_computation.82 | convolution fusion | flops 83230720 | bytes 5206016 | tf_op jit(solution)/shard_map/dot_general | solution.py:22
  35.4 2.3 %copy.59 = bf16[32,40,8,128]{3,0,2,1:T(8,128)(2,1)} copy(bf16[32,40,8,128]{3,0,1,2:T(8,128)(2,1)S(1)} %multiply_convert_fusion) | data formatting | bytes 5242880 | tf_op jit(solution)/shard_map/convert_element_type | solution.py:16
  37.7 0.7 copy.73
  38.4 1.4 %copy.70 = f32[32,32]{0,1:T(8,128)} copy(f32[32,32]{1,0:T(8,128)} %fusion.136) | data formatting | bytes 8192 | tf_op jit(solution)/shard_map/dot_general | solution.py:22
  39.8 2.1 %collective-permute-start.5 = (bf16[32,1,8,128]{3,0,1,2:T(8,128)(2,1)S(1)}, bf16[32,1,8,128]{3,0,1,2:T(8,128)(2,1)S(1)}, u32[]{:S(2)}, u32[]{:S(2)}) collective-permute-start(bf16[32,1,8,128]{3,0,1,2:T(8,128)(2,1)S(1)} %get-tuple-element.9), channel_id=1, source_target_pairs={{8,0},{16,8},{24,16},{32,24},{40,32},{48,40},{56,48},{64,56},{72,6... | collective-permute-start | bytes 196616 | tf_op jit(solution)/shard_map/ppermute | solution.py:12
  41.9 0.7 bitcast_convert_fusion
  42.6 0.9 multiply_convert_fusion.3
  43.4 0.8 fusion.133
  44.2 0.7 bitcast_convert_fusion.1
  44.9 0.9 multiply_convert_fusion.4
  45.8 0.8 fusion.154
  46.6 0.9 fusion.180
  47.5 1.4 %fusion.148 = f32[1,32,32]{2,1,0:T(8,128)} fusion(f32[32,32]{1,0:T(8,128)S(1)} %fusion.149, f32[32,32]{1,0:T(8,128)S(1)} %copy-done.10, f32[32,32]{1,0:T(8,128)S(1)} %fusion.133, f32[32,32]{1,0:T(8,128)S(1)} %fusion.154, f32[32,32]{0,1:T(8,128)S(1)} %copy-done.11, f32[32,32]{0,1:T(8,128)S(1)} %copy-done.12, ...), kind=kOutput, calls=%fused_computation.91 | convolution fusion | flops 83893248 | bytes 2650112 | tf_op jit(solution)/shard_map/dot_general | solution.py:22
  49.0 1.6 %multiply_convert_fusion.1 = bf16[32,16,8,128]{3,0,1,2:T(8,128)(2,1)S(1)} fusion(bf16[32,16,8,128]{3,0,1,2:T(8,128)(2,1)} %collective-permute-done.4, f32[16,8,128]{2,0,1:T(8,128)S(1)} %copy.88), kind=kLoop, calls=%fused_computation.31 | loop fusion | flops 1572864 | bytes 2162688 | tf_op jit(solution)/shard_map/convert_element_type | solution.py:16
  50.7 0.2 copy-done.1
  50.9 2.7 %maximum_maximum_fusion = (bf16[64,19,8,128]{3,0,1,2:T(8,128)(2,1)S(1)}, bf16[64,19,8,128]{3,0,1,2:T(8,128)(2,1)S(1)}) fusion(bf16[32,2,8,128]{3,0,1,2:T(8,128)(2,1)S(1)} %broadcast_in_dim.28, bf16[32,1,8,128]{3,0,1,2:T(8,128)(2,1)S(1)} %collective-permute-done.2, bf16[32,18,8,128]{3,0,1,2:T(8,128)(2,1)S(1)} %copy-done, ...), kind=kLoop, calls=%fused_computation.12 | loop fusion | flops 26476544 | bytes 9895936 | tf_op jit(solution)/shard_map/concatenate | solution.py:70
  53.6 3.3 %fusion.169 = (bf16[64,17,7,128]{3,0,1,2:T(8,128)(2,1)}, bf16[64,17,7,128]{3,0,1,2:T(8,128)(2,1)}, bf16[64,17,7,128]{3,0,1,2:T(8,128)(2,1)S(1)}, bf16[64,17,7,128]{3,0,1,2:T(8,128)(2,1)S(1)}) fusion(bf16[64,19,8,128]{3,0,1,2:T(8,128)(2,1)S(1)} %get-tuple-element.34, bf16[64,19,8,128]{3,0,1,2:T(8,128)(2,1)S(1)} %get-tuple-element.35), kind=kLoop, calls=%fused_computation.149 | loop fusion | bytes 15597568 | tf_op jit(solution)/shard_map/slice | solution.py:36
  56.9 4.4 %fusion.168 = (bf16[64,17,8,127]{3,0,1,2:T(8,128)(2,1)}, bf16[64,17,8,127]{3,0,1,2:T(8,128)(2,1)}, bf16[64,17,8,127]{3,0,1,2:T(8,128)(2,1)}, bf16[64,17,8,127]{3,0,1,2:T(8,128)(2,1)}) fusion(bf16[64,19,8,128]{3,0,1,2:T(8,128)(2,1)S(1)} %get-tuple-element.34, bf16[64,19,8,128]{3,0,1,2:T(8,128)(2,1)S(1)} %get-tuple-element.35), kind=kLoop, calls=%fused_computation.148 | loop fusion | bytes 17686528 | tf_op jit(solution)/shard_map/slice | solution.py:35
  61.3 5.8 %fusion.167 = (bf16[64,17,8,128]{3,0,1,2:T(8,128)(2,1)}, bf16[64,17,8,128]{3,0,1,2:T(8,128)(2,1)}, bf16[64,17,8,128]{3,0,1,2:T(8,128)(2,1)}, bf16[64,17,8,128]{3...) fusion(bf16[64,19,8,128]{3,0,1,2:T(8,128)(2,1)S(1)} %get-tuple-element.34, ...), kind=kLoop, calls=%fused_computation.147 | loop fusion | bytes 26738688 | tf_op jit(solution)/shard_map/slice | solution.py:32
  67.1 1.5 %multiply_convert_fusion.2 = bf16[32,16,8,128]{3,0,2,1:T(8,128)(2,1)S(1)} fusion(bf16[32,16,8,128]{3,0,2,1:T(8,128)(2,1)} %collective-permute-done.3, f32[16,8,128]{2,1,0:T(8,128)S(1)} %get-tuple-element.38), kind=kLoop, calls=%fused_computation.32 | loop fusion | flops 1572864 | bytes 2162688 | tf_op jit(solution)/shard_map/convert_element_type | solution.py:16
  68.7 2.7 %collective-permute-start.6 = (bf16[96,40,128]{2,0,1:T(8,128)(2,1)S(1)}, bf16[96,40,128]{2,0,1:T(8,128)(2,1)}, u32[]{:S(2)}, u32[]{:S(2)}) collective-permute-start(bf16[96,40,128]{2,0,1:T(8,128)(2,1)S(1)} %fusion.158), channel_id=1, source_target_pairs={{0,1},{1,2},{2,3},{3,4},{4,5},{5,6},{6,7},{8,9},{9,10},{10,11},{11... | collective-permute-start | bytes 2949128 | tf_op jit(solution)/shard_map/ppermute | solution.py:12
  71.4 0.9 slice_bitcast_fusion.8
  72.4 4.1 %collective-permute-start.7 = (bf16[96,40,128]{2,0,1:T(8,128)(2,1)S(1)}, bf16[96,40,128]{2,0,1:T(8,128)(2,1)S(1)}, u32[]{:S(2)}, u32[]{:S(2)}) collective-permute-start(bf16[96,40,128]{2,0,1:T(8,128)(2,1)S(1)} %fusion.156), channel_id=1, source_target_pairs={{1,0},{2,1},{3,2},{4,3},{5,4},{6,5},{7,6},{9,8},{10,9},{11,10},{12... | collective-permute-start | bytes 2949128 | tf_op jit(solution)/shard_map/ppermute | solution.py:12
  76.5 0.6 fusion.56
  77.2 2.8 %fusion.51 = f32[64,64]{1,0:T(8,128)S(1)} fusion(bf16[64,17,7,128]{3,0,1,2:T(8,128)(2,1)} %get-tuple-element.18, bf16[64,17,7,128]{3,0,1,2:T(8,128)(2,1)} %get-tuple-element.17), kind=kOutput, calls=%fused_computation.59 | convolution fusion | flops 124780544 | bytes 3915776 | tf_op jit(solution)/shard_map/dot_general | solution.py:22
  80.1 3.0 %fusion.86 = f32[64,64]{1,0:T(8,128)S(1)} fusion(bf16[64,17,8,127]{3,0,1,2:T(8,128)(2,1)} %get-tuple-element.53, bf16[64,17,8,127]{3,0,1,2:T(8,128)(2,1)} %get-tuple-element.54), kind=kOutput, calls=%fused_computation.66 | convolution fusion | flops 141492224 | bytes 4438016 | tf_op jit(solution)/shard_map/dot_general | solution.py:22
  83.2 3.0 %fusion.71 = f32[64,64]{1,0:T(8,128)S(1)} fusion(bf16[64,17,8,127]{3,0,1,2:T(8,128)(2,1)} %get-tuple-element.16, bf16[64,17,8,127]{3,0,1,2:T(8,128)(2,1)} %get-tuple-element.15), kind=kOutput, calls=%fused_computation.63 | convolution fusion | flops 141492224 | bytes 4438016 | tf_op jit(solution)/shard_map/dot_general | solution.py:22
  86.4 3.2 %fusion.61 = f32[64,64]{1,0:T(8,128)S(1)} fusion(bf16[64,17,8,128]{3,0,1,2:T(8,128)(2,1)} %get-tuple-element.12, bf16[64,17,8,128]{3,0,1,2:T(8,128)(2,1)} %get-tuple-element.14), kind=kOutput, calls=%fused_computation.61 | convolution fusion | flops 142606336 | bytes 4472832 | tf_op jit(solution)/shard_map/dot_general | solution.py:22
  89.5 0.5 copy-done.8
  90.0 0.7 fusion.66
  90.7 0.9 copy-done.4
  91.6 0.7 copy-done.7
  92.3 0.7 fusion.81
  93.0 0.9 copy-done.6
  93.9 0.7 fusion.76
  94.7 0.7 fusion.130
  95.4 0.7 fusion.109
  96.4 1.6 %fusion.44 = f32[96,96]{1,0:T(8,128)S(1)} fusion(bf16[96,40,128]{2,0,1:T(8,128)(2,1)S(1)} %fusion.156, bf16[96,40,128]{2,0,1:T(8,128)(2,1)} %collective-permute-done.6), kind=kOutput, calls=%fused_computation.56 | convolution fusion | flops 94381056 | bytes 2002944 | tf_op jit(solution)/shard_map/dot_general | solution.py:22
  98.0 0.1 reshape.89
  98.1 0.4 fusion.43
  98.8 6.3 %collective-permute-start.8 = (f32[3,3,32,32]{3,2,1,0:T(8,128)S(1)}, f32[3,3,32,32]{3,2,1,0:T(8,128)S(1)}, u32[]{:S(2)}, u32[]{:S(2)}) collective-permute-start(f32[3,3,32,32]{3,2,1,0:T(8,128)S(1)} %get-tuple-element.28), channel_id=1, source_target_pairs={{0,8},{8,16},{16,24},{24,32},{32,40},{40,48},{48,56},{56,64},{64,7... | collective-permute-start | bytes 110600 | tf_op jit(solution)/shard_map/ppermute | solution.py:12
  105.1 1.9 %collective-permute-start.9 = (f32[3,3,32,32]{3,2,1,0:T(8,128)S(1)}, f32[3,3,32,32]{3,2,1,0:T(8,128)S(1)}, u32[]{:S(2)}, u32[]{:S(2)}) collective-permute-start(f32[3,3,32,32]{3,2,1,0:T(8,128)S(1)} %get-tuple-element.30), channel_id=1, source_target_pairs={{8,0},{16,8},{24,16},{32,24},{40,32},{48,40},{56,48},{64,56},{72,6... | collective-permute-start | bytes 110600 | tf_op jit(solution)/shard_map/ppermute | solution.py:12
  107.0 0.2 collective-permute-done.8
  107.2 6.5 %collective-permute-done.9 = f32[3,3,32,32]{3,2,1,0:T(8,128)S(1)} collective-permute-done((f32[3,3,32,32]{3,2,1,0:T(8,128)S(1)}, f32[3,3,32,32]{3,2,1,0:T(8,128)S(1)}, u32[]{:S(2)}, u32[]{:S(2)}) %collective-permute-start.9) | collective-permute-done | bytes 36896 | tf_op jit(solution)/shard_map/ppermute | solution.py:12
  113.7 0.6 maximum_bitcast_fusion.1
  114.3 0.6 fusion.159
  (57 shorter events, 1.2 us)
Async XLA Ops:
  0.6 17.0 %copy-start.9 = (bf16[32,16,8,128]{3,2,1,0:T(8,128)(2,1)S(1)}, bf16[32,16,8,128]{3,2,1,0:T(8,128)(2,1)}, u32[]{:S(2)}) copy-start(bf16[32,16,8,128]{3,2,1,0:T(8,128)(2,1)} %param.8) | copy-start | bytes 3145732
  3.1 36.6 %collective-permute-start.1 = (bf16[1,8,128]{2,1,0:T(8,128)(2,1)}, bf16[1,8,128]{2,1,0:T(8,128)(2,1)}, u32[]{:S(2)}, u32[]{:S(2)}) collective-permute-start(bf16[1,8,128]{2,1,0:T(8,128)(2,1)} %get-tuple-element.36), channel_id=1, source_target_pairs={{0,8},{8,16},{16,24},{24,32},{32,40},{40,48},{48,56},{56,64},{64,7... | collective-permute-start | bytes 6152 | tf_op jit(solution)/shard_map/ppermute | solution.py:12
  6.5 17.7 %copy-start.2 = (bf16[32,40,8,128]{3,2,1,0:T(8,128)(2,1)S(1)}, bf16[32,40,8,128]{3,2,1,0:T(8,128)(2,1)}, u32[]{:S(2)}) copy-start(bf16[32,40,8,128]{3,2,1,0:T(8,128)(2,1)} %param.6) | copy-start | bytes 7864324
  6.5 37.7 %collective-permute-start = (bf16[1,8,128]{2,1,0:T(8,128)(2,1)}, bf16[1,8,128]{2,1,0:T(8,128)(2,1)}, u32[]{:S(2)}, u32[]{:S(2)}) collective-permute-start(bf16[1,8,128]{2,1,0:T(8,128)(2,1)} %get-tuple-element.37), channel_id=1, source_target_pairs={{8,0},{16,8},{24,16},{32,24},{40,32},{48,40},{56,48},{64,56},{72,6... | collective-permute-start | bytes 6152 | tf_op jit(solution)/shard_map/ppermute | solution.py:12
  14.1 34.9 %collective-permute-start.4 = (bf16[32,16,8,128]{3,0,1,2:T(8,128)(2,1)}, bf16[32,16,8,128]{3,0,1,2:T(8,128)(2,1)}, u32[]{:S(2)}, u32[]{:S(2)}) collective-permute-start(bf16[32,16,8,128]{3,0,1,2:T(8,128)(2,1)} %copy_select_fusion), channel_id=1, source_target_pairs={{8,0},{16,8},{24,16},{32,24},{40,32},{48,40},{56,48},{64,56},{72,6... | collective-permute-start | bytes 3145736 | tf_op jit(solution)/shard_map/ppermute | solution.py:12
  19.3 31.3 %collective-permute-start.3 = (bf16[32,16,8,128]{3,0,2,1:T(8,128)(2,1)}, bf16[32,16,8,128]{3,0,2,1:T(8,128)(2,1)}, u32[]{:S(2)}, u32[]{:S(2)}) collective-permute-start(bf16[32,16,8,128]{3,0,2,1:T(8,128)(2,1)} %copy_select_fusion.1), channel_id=1, source_target_pairs={{0,8},{8,16},{16,24},{24,32},{32,40},{40,48},{48,56},{56,64},{64,7... | collective-permute-start | bytes 3145736 | tf_op jit(solution)/shard_map/ppermute | solution.py:12
  26.7 23.9 %collective-permute-start.2 = (bf16[32,1,8,128]{3,0,1,2:T(8,128)(2,1)}, bf16[32,1,8,128]{3,0,1,2:T(8,128)(2,1)S(1)}, u32[]{:S(2)}, u32[]{:S(2)}) collective-permute-start(bf16[32,1,8,128]{3,0,1,2:T(8,128)(2,1)} %get-tuple-element.8), channel_id=1, source_target_pairs={{0,8},{8,16},{16,24},{24,32},{32,40},{40,48},{48,56},{56,64},{64,7... | collective-permute-start | bytes 196616 | tf_op jit(solution)/shard_map/ppermute | solution.py:12
  39.8 10.9 %collective-permute-start.5 = (bf16[32,1,8,128]{3,0,1,2:T(8,128)(2,1)S(1)}, bf16[32,1,8,128]{3,0,1,2:T(8,128)(2,1)S(1)}, u32[]{:S(2)}, u32[]{:S(2)}) collective-permute-start(bf16[32,1,8,128]{3,0,1,2:T(8,128)(2,1)S(1)} %get-tuple-element.9), channel_id=1, source_target_pairs={{8,0},{16,8},{24,16},{32,24},{40,32},{48,40},{56,48},{64,56},{72,6... | collective-permute-start | bytes 196616 | tf_op jit(solution)/shard_map/ppermute | solution.py:12
  43.4 2.4 %copy-start.3 = (bf16[32,40,8,128]{3,0,2,1:T(8,128)(2,1)S(1)}, bf16[32,40,8,128]{3,0,2,1:T(8,128)(2,1)}, u32[]{:S(2)}) copy-start(bf16[32,40,8,128]{3,0,2,1:T(8,128)(2,1)} %copy.59) | copy-start | bytes 7864324
  45.8 1.7 %copy-start.10 = (f32[32,32]{1,0:T(8,128)S(1)}, f32[32,32]{1,0:T(8,128)}, u32[]{:S(2)}) copy-start(f32[32,32]{1,0:T(8,128)} %fusion.136) | copy-start | bytes 12292
  45.8 1.7 %copy-start.11 = (f32[32,32]{0,1:T(8,128)S(1)}, f32[32,32]{0,1:T(8,128)}, u32[]{:S(2)}) copy-start(f32[32,32]{0,1:T(8,128)} %copy.73) | copy-start | bytes 12292
  45.8 1.7 %copy-start.12 = (f32[32,32]{0,1:T(8,128)S(1)}, f32[32,32]{0,1:T(8,128)}, u32[]{:S(2)}) copy-start(f32[32,32]{0,1:T(8,128)} %copy.70) | copy-start | bytes 12292
  49.0 1.7 %copy-start = (bf16[32,18,8,128]{3,0,1,2:T(8,128)(2,1)S(1)}, bf16[32,18,8,128]{3,0,1,2:T(8,128)(2,1)}, u32[]{:S(2)}) copy-start(bf16[32,18,8,128]{3,0,1,2:T(8,128)(2,1)} %get-tuple-element.6) | copy-start | bytes 3538948
  49.0 1.9 %copy-start.1 = (bf16[32,18,8,128]{3,0,1,2:T(8,128)(2,1)S(1)}, bf16[32,18,8,128]{3,0,1,2:T(8,128)(2,1)}, u32[]{:S(2)}) copy-start(bf16[32,18,8,128]{3,0,1,2:T(8,128)(2,1)} %get-tuple-element.7) | copy-start | bytes 3538948
  68.7 27.6 %collective-permute-start.6 = (bf16[96,40,128]{2,0,1:T(8,128)(2,1)S(1)}, bf16[96,40,128]{2,0,1:T(8,128)(2,1)}, u32[]{:S(2)}, u32[]{:S(2)}) collective-permute-start(bf16[96,40,128]{2,0,1:T(8,128)(2,1)S(1)} %fusion.158), channel_id=1, source_target_pairs={{0,1},{1,2},{2,3},{3,4},{4,5},{5,6},{6,7},{8,9},{9,10},{10,11},{11... | collective-permute-start | bytes 2949128 | tf_op jit(solution)/shard_map/ppermute | solution.py:12
  72.4 25.7 %collective-permute-start.7 = (bf16[96,40,128]{2,0,1:T(8,128)(2,1)S(1)}, bf16[96,40,128]{2,0,1:T(8,128)(2,1)S(1)}, u32[]{:S(2)}, u32[]{:S(2)}) collective-permute-start(bf16[96,40,128]{2,0,1:T(8,128)(2,1)S(1)} %fusion.156), channel_id=1, source_target_pairs={{1,0},{2,1},{3,2},{4,3},{5,4},{6,5},{7,6},{9,8},{10,9},{11,10},{12... | collective-permute-start | bytes 2949128 | tf_op jit(solution)/shard_map/ppermute | solution.py:12
  86.4 3.2 %copy-start.5 = (bf16[64,17,8,128]{3,0,1,2:T(8,128)(2,1)S(1)}, bf16[64,17,8,128]{3,0,1,2:T(8,128)(2,1)}, u32[]{:S(2)}) copy-start(bf16[64,17,8,128]{3,0,1,2:T(8,128)(2,1)} %get-tuple-element.14) | copy-start | bytes 6684676
  86.4 3.6 %copy-start.8 = (bf16[64,17,8,128]{3,0,1,2:T(8,128)(2,1)S(1)}, bf16[64,17,8,128]{3,0,1,2:T(8,128)(2,1)}, u32[]{:S(2)}) copy-start(bf16[64,17,8,128]{3,0,1,2:T(8,128)(2,1)} %get-tuple-element.13) | copy-start | bytes 6684676
  90.0 1.6 %copy-start.4 = (bf16[64,17,8,128]{3,0,1,2:T(8,128)(2,1)S(1)}, bf16[64,17,8,128]{3,0,1,2:T(8,128)(2,1)}, u32[]{:S(2)}) copy-start(bf16[64,17,8,128]{3,0,1,2:T(8,128)(2,1)} %get-tuple-element.50) | copy-start | bytes 6684676
  90.0 2.3 %copy-start.7 = (bf16[64,17,8,128]{3,0,1,2:T(8,128)(2,1)S(1)}, bf16[64,17,8,128]{3,0,1,2:T(8,128)(2,1)}, u32[]{:S(2)}) copy-start(bf16[64,17,8,128]{3,0,1,2:T(8,128)(2,1)} %get-tuple-element.51) | copy-start | bytes 6684676
  92.3 1.6 %copy-start.6 = (bf16[64,17,8,128]{3,0,1,2:T(8,128)(2,1)S(1)}, bf16[64,17,8,128]{3,0,1,2:T(8,128)(2,1)}, u32[]{:S(2)}) copy-start(bf16[64,17,8,128]{3,0,1,2:T(8,128)(2,1)} %get-tuple-element.52) | copy-start | bytes 6684676
  95.4 0.9 copy-start.13
  98.8 8.4 %collective-permute-start.8 = (f32[3,3,32,32]{3,2,1,0:T(8,128)S(1)}, f32[3,3,32,32]{3,2,1,0:T(8,128)S(1)}, u32[]{:S(2)}, u32[]{:S(2)}) collective-permute-start(f32[3,3,32,32]{3,2,1,0:T(8,128)S(1)} %get-tuple-element.28), channel_id=1, source_target_pairs={{0,8},{8,16},{16,24},{24,32},{32,40},{40,48},{48,56},{56,64},{64,7... | collective-permute-start | bytes 110600 | tf_op jit(solution)/shard_map/ppermute | solution.py:12
  105.1 8.6 %collective-permute-start.9 = (f32[3,3,32,32]{3,2,1,0:T(8,128)S(1)}, f32[3,3,32,32]{3,2,1,0:T(8,128)S(1)}, u32[]{:S(2)}, u32[]{:S(2)}) collective-permute-start(f32[3,3,32,32]{3,2,1,0:T(8,128)S(1)} %get-tuple-element.30), channel_id=1, source_target_pairs={{8,0},{16,8},{24,16},{32,24},{40,32},{48,40},{56,48},{64,56},{72,6... | collective-permute-start | bytes 110600 | tf_op jit(solution)/shard_map/ppermute | solution.py:12
where the time goes:
time: 116 us; the launch traced here: 115 us
  starting transfers between devices  32.6 us (28%)
  local copies, waits for them, and re-layouts  28.6 us (25%)
  matrix products  23.5 us (20%)
  other arithmetic  21.7 us (19%)
  waiting for transfers between devices  6.66 us (6%)
  between operations  1.87 us (2%)
    ppermute x10, starting transfers between devices, shifted(): lax.ppermute(value, axis, [(source, source + steps) for source in range(i...  32.6 us
    dot_general x17, matrix products, pair_gram(): lax.dot_general(left_flat, right_flat, (((1,), (1,)), ((), ())), preferre...  23.5 us
    convert_element_type x6, other arithmetic, scaled(): (factor.astype(jnp.float32) * values.astype(jnp.float32)).astype(jnp.bflo...  7.63 us
    ppermute x10, waiting for transfers between devices, shifted(): lax.ppermute(value, axis, [(source, source + steps) for source in range(i...  6.66 us
    slice x1, local copies, waits for them, and re-layouts, energy(): field_planes[:, 2:]  5.81 us
    slice x2, local copies, waits for them, and re-layouts, energy(): north_pairs = pair_gram(inner_cells[:, :, :, :-1], inner_cells[:, :, :, 1:])  5.58 us
    slice x2, local copies, waits for them, and re-layouts, energy(): depth_pairs = pair_gram(inner_cells[:, :, :-1], inner_cells[:, :, 1:])  4.28 us
    select_n x1, other arithmetic, keep_margins(): jnp.where(plane_index >= left_part.shape[1] - widths[0], left_part, jnp.z...  3.43 us
  transfers between devices with their start and end apart: 10, of which 2 were waited for; matrix products, arithmetic and copies ran while one was open for 42% of the time, Pallas kernels for 0%

commit v1 on v0

v1 whole, which is shorter than its diff:
```python
import functools

import jax
import jax.numpy as jnp
from jax import lax
from jax.experimental import pallas as pl
from jax.experimental.pallas import tpu as pltpu
from jax.sharding import PartitionSpec as P

MESH = pl.DeviceIdType.MESH
f32 = jnp.float32
bf16 = jnp.bfloat16
diagonal_weight = 6.1

CHUNKS = 4

STRIP_R, STRIP_L, EDGE_R, OWN_UP, OWN_DOWN, MARGIN_UP, MARGIN_DOWN, PART_R, PART_L, PART_UP, PART_DOWN = range(11)
BULK_R = 11
BULK_L = BULK_R + CHUNKS
REMOTE = BULK_L + CHUNKS

PERM, MASK, WIDTH, LEFT, RIGHT, OWN = range(6)


def nt(left, right):
    return lax.dot_general(left, right, (((1,), (1,)), ((), ())), preferred_element_type=f32)


def nn(left, right):
    return jnp.dot(left, right, preferred_element_type=f32)


def split(value):
    high = value.astype(bf16)
    return high, (value - high.astype(f32)).astype(bf16)


def kernel(
    lat_n, depth_n,
    own_hbm, left_hbm, right_hbm, perm_hbm, mask_hbm, width_hbm,
    lateral_ref, vertical_ref,
    own_v, left_v, right_v, perm_v, mask_v, width_s,
    scale_v, strip_out, strip_in, factor_v,
    field_v, high_v, low_v, edge_in,
    margin_v, mhigh_v, mlow_v,
    land_v, other_v,
    planes_v, above_v, mplanes_v, mabove_v,
    acc_v, part_out, part_in,
    local_sem, send_sem, recv_sem,
):
    basis, cells, layers, north = own_hbm.shape
    margin = left_hbm.shape[1]
    rows = basis * layers
    lat, dep = lax.axis_index("lat"), lax.axis_index("depth")
    right = (lax.rem(lat + 1, lat_n), dep)
    left = (lax.rem(lat + lat_n - 1, lat_n), dep)
    up = (lat, lax.rem(dep + 1, depth_n))
    down = (lat, lax.rem(dep + depth_n - 1, depth_n))

    def remote(index, src, dst, device):
        return pltpu.make_async_remote_copy(
            src_ref=src, dst_ref=dst, send_sem=send_sem.at[index], recv_sem=recv_sem.at[index],
            device_id=device, device_id_type=MESH,
        )

    def columns(plane, count):
        return pl.ds(pl.multiple_of(plane * north, north), count * north)

    barrier = pltpu.get_barrier_semaphore()
    for device in (right, left, up, down):
        pl.semaphore_signal(barrier, inc=1, device_id=device, device_id_type=MESH)

    local = [
        pltpu.make_async_copy(perm_hbm, perm_v, local_sem.at[PERM]),
        pltpu.make_async_copy(mask_hbm, mask_v, local_sem.at[MASK]),
        pltpu.make_async_copy(width_hbm, width_s, local_sem.at[WIDTH]),
        pltpu.make_async_copy(left_hbm, left_v, local_sem.at[LEFT]),
        pltpu.make_async_copy(right_hbm, right_v, local_sem.at[RIGHT]),
        pltpu.make_async_copy(own_hbm, own_v, local_sem.at[OWN]),
    ]
    for index in (PERM, MASK, WIDTH, OWN, LEFT, RIGHT):
        local[index].start()
    for index in (PERM, MASK, WIDTH):
        local[index].wait()

    factor = 0.05 + 0.95 * mask_v[...].astype(f32)
    scaling = jnp.sqrt(perm_v[...] * factor[:, :, None]).astype(bf16)
    scale_v[...] = scaling.astype(f32)
    left_width, right_width = width_s[0, 0, 0], width_s[0, 0, 1]
    strip_out[0, 0:margin] = scaling[cells - margin :]
    strip_out[0, margin] = jnp.full((layers, north), right_width.astype(f32), f32).astype(bf16)
    strip_out[1, 0:margin] = scaling[:margin]
    strip_out[1, margin] = jnp.full((layers, north), left_width.astype(f32), f32).astype(bf16)

    pl.semaphore_wait(barrier, 4)
    strip_r = remote(STRIP_R, strip_out.at[0], strip_in.at[0], right)
    strip_l = remote(STRIP_L, strip_out.at[1], strip_in.at[1], left)
    strip_r.start()
    strip_l.start()
    size = margin // CHUNKS
    bulk_r, bulk_l = [], []
    for c in range(CHUNKS):
        part = pl.ds(c * size, size)
        bulk_r.append(remote(BULK_R + c, right_hbm.at[:, part], land_v.at[0, :, part], right))
        bulk_l.append(remote(BULK_L + c, left_hbm.at[:, part], land_v.at[1, :, part], left))
        bulk_r[c].start()
        bulk_l[c].start()

    pick_row = lax.broadcasted_iota(jnp.int32, (2 * basis, rows), 0)
    pick_col = lax.broadcasted_iota(jnp.int32, (2 * basis, rows), 1)
    wanted = jnp.where(pick_row < basis, pick_row * layers + layers - 1, (pick_row - basis) * layers)
    pick = (pick_col == wanted).astype(f32).astype(bf16)

    lane = lax.broadcasted_iota(jnp.int32, (rows, north), 1)
    layer = lax.rem(lax.broadcasted_iota(jnp.int32, (rows, north), 0), layers)
    zero_plane = jnp.zeros((rows, north), bf16)
    field_v[:, 0:north] = zero_plane
    field_v[:, (cells + 1) * north : (cells + 2) * north] = zero_plane

    def scaled(values, factors):
        return (values.astype(f32) * factors[None]).reshape(rows, north).astype(bf16)

    local[OWN].wait()
    group = 4

    def own_group(step, _):
        first = step * group
        for j in range(group):
            field_v[:, columns(first + 1 + j, 1)] = scaled(own_v[:, first + j], scale_v[first + j])
        planes_v[:, columns(first, group)] = nn(pick, field_v[:, columns(first + 1, group)]).astype(bf16)
        return _

    lax.fori_loop(0, cells // group, own_group, 0)
    own_up = remote(OWN_UP, planes_v.at[0:basis], above_v.at[basis : 2 * basis], up)
    own_down = remote(OWN_DOWN, planes_v.at[basis : 2 * basis], above_v.at[0:basis], down)
    own_up.start()
    own_down.start()
    edge_r = remote(EDGE_R, field_v.at[:, pl.ds(cells * north, north)], edge_in, right)
    edge_r.start()

    strip_r.wait_recv()
    strip_l.wait_recv()
    at = lax.broadcasted_iota(jnp.int32, (margin, layers, north), 0).astype(f32)
    zero_factor = jnp.zeros((margin, layers, north), f32)
    from_left = strip_in[0].astype(f32)
    from_right = strip_in[1].astype(f32)
    factor_v[0] = jnp.where(at >= margin - left_width.astype(f32), from_left[:margin], zero_factor)
    factor_v[1] = jnp.where(at < right_width.astype(f32), from_right[:margin], zero_factor)
    factor_v[2] = jnp.where(at < from_left[margin:], scale_v[0:margin], zero_factor)
    factor_v[3] = jnp.where(at >= margin - from_right[margin:], scale_v[cells - margin : cells], zero_factor)

    local[LEFT].wait()
    local[RIGHT].wait()
    for side, source in ((0, left_v), (1, right_v)):
        margin_v[side, :, margin * north : (margin + 1) * north] = zero_plane

        def margin_group(step, _, side=side, source=source):
            first = step * group
            for j in range(group):
                margin_v[side, :, columns(first + j, 1)] = scaled(source[:, first + j], factor_v[side, first + j])
            mplanes_v[side, :, columns(first, group)] = nn(
                pick, margin_v[side, :, columns(first, group)]
            ).astype(bf16)
            return _

        lax.fori_loop(0, margin // group, margin_group, 0)
    margin_up = remote(MARGIN_UP, mplanes_v.at[0, 0:basis], mabove_v.at[0], up)
    margin_down = remote(MARGIN_DOWN, mplanes_v.at[1, basis : 2 * basis], mabove_v.at[1], down)
    margin_up.start()
    margin_down.start()

    zero = jnp.zeros((rows, north), f32)

    def sublane_roll(value, shift):
        return pltpu.roll(value.reshape(basis, layers, north), shift, 1).reshape(rows, north)

    def own_operator(plane, _):
        here = field_v[:, columns(plane + 1, 1)].astype(f32)
        east = field_v[:, columns(plane, 1)].astype(f32) + field_v[:, columns(plane + 2, 1)].astype(f32)
        sides = jnp.where(lane > 0, pltpu.roll(here, 1, 1), zero) + jnp.where(
            lane < north - 1, pltpu.roll(here, north - 1, 1), zero
        )
        ends = jnp.where(layer > 0, sublane_roll(here, 1), zero) + jnp.where(
            layer < layers - 1, sublane_roll(here, layers - 1), zero
        )
        high, low = split(diagonal_weight * here - east - sides - ends)
        high_v[:, columns(plane, 1)] = high
        low_v[:, columns(plane, 1)] = low
        return _

    lax.fori_loop(0, cells, own_operator, 0)

    for side in range(2):

        def margin_operator(plane, _, side=side):
            here = margin_v[side, :, columns(plane, 1)].astype(f32)
            east = margin_v[side, :, columns(plane + 1, 1)].astype(f32)
            sides = jnp.where(lane < north - 1, pltpu.roll(here, north - 1, 1), zero)
            ends = jnp.where(layer < layers - 1, sublane_roll(here, layers - 1), zero)
            high, low = split(diagonal_weight * here - 2.0 * (east + sides + ends))
            mhigh_v[side, :, columns(plane, 1)] = high
            mlow_v[side, :, columns(plane, 1)] = low
            return _

        lax.fori_loop(0, margin, margin_operator, 0)

    first_edge = jnp.concatenate([field_v[:, north : 2 * north], field_v[:, cells * north : (cells + 1) * north]], 1)
    last_edge = jnp.concatenate(
        [margin_v[0, :, (margin - 1) * north : margin * north], margin_v[1, :, 0:north]], 1
    )
    acc_v[0] = nt(first_edge, -2.0 * last_edge)
    run = 8

    def own_gram(step, _):
        fields = field_v[:, columns(step * run + 1, run)]
        acc_v[0] += nt(fields, high_v[:, columns(step * run, run)]) + nt(fields, low_v[:, columns(step * run, run)])
        return _

    lax.fori_loop(0, cells // run, own_gram, 0)
    for side in range(2):

        def margin_gram(step, _, side=side):
            fields = margin_v[side, :, columns(step * run, run)]
            acc_v[0] += nt(fields, mhigh_v[side, :, columns(step * run, run)]) + nt(
                fields, mlow_v[side, :, columns(step * run, run)]
            )
            return _

        lax.fori_loop(0, margin // run, margin_gram, 0)

    same_layer = (
        lax.rem(lax.broadcasted_iota(jnp.int32, (rows, rows), 0), layers)
        == lax.rem(lax.broadcasted_iota(jnp.int32, (rows, rows), 1), layers)
    )
    gather = (
        lax.broadcasted_iota(jnp.int32, (rows, basis), 0) // layers
        == lax.broadcasted_iota(jnp.int32, (rows, basis), 1)
    ).astype(f32)

    def collapse(matrix):
        kept = jnp.where(same_layer, matrix, jnp.zeros_like(matrix))
        summed = jnp.sum(kept.reshape(basis, layers, rows), axis=1)
        return jnp.dot(summed, gather, precision=lax.Precision.HIGHEST, preferred_element_type=f32)

    own_block = collapse(acc_v[0])
    own_block = 0.5 * (own_block + own_block.T)

    own_up.wait_recv()
    own_down.wait_recv()
    across = nt(planes_v[...], above_v[...])
    margin_up.wait_recv()
    margin_down.wait_recv()
    left_bottom = mplanes_v[0, basis : 2 * basis]
    right_top = mplanes_v[1, 0:basis]
    across_down = across[basis:, basis:] + nt(left_bottom, mabove_v[0])
    across_up = across[:basis, :basis] + nt(right_top, mabove_v[1])
    margin_to_down = nt(mabove_v[0], left_bottom)
    margin_to_up = nt(mabove_v[1], right_top)

    edge_r.wait_recv()
    far_edge = edge_in[...]
    starts = (0, cells - margin)
    totals = [None, None]
    pairs = [None, None]
    pairs_t = [None, None]
    for c in range(CHUNKS):
        for side, bulk in ((0, bulk_r), (1, bulk_l)):
            bulk[c].wait_recv()
            for j in range(size):
                plane = c * size + j
                other_v[side, :, plane * north : (plane + 1) * north] = scaled(
                    land_v[side, :, plane], factor_v[2 + side, plane]
                )
            other = other_v[side, :, c * size * north : (c + 1) * size * north]
            span = pl.ds((starts[side] + c * size) * north, size * north)
            term = nt(other, high_v[:, span]) + nt(other, low_v[:, span])
            if side == 0 and c == 0:
                far = jnp.concatenate([far_edge, other[:, :north]], 1)
                near = jnp.concatenate(
                    [field_v[:, north : 2 * north], margin_v[0, :, (margin - 1) * north : margin * north]], 1
                )
                term = term + nt(far, -near)
            if c == 0:
                acc_v[1 + side] = term
            else:
                acc_v[1 + side] += term
            other_planes = nn(pick, other).astype(bf16)
            above = above_v[:, span]
            pair, pair_t = nt(above, other_planes), nt(other_planes, above)
            pairs[side] = pair if c == 0 else pairs[side] + pair
            pairs_t[side] = pair_t if c == 0 else pairs_t[side] + pair_t

    blank = jnp.zeros((basis, basis), f32)
    with_left, with_right = pairs
    part_out[2] = jnp.concatenate([with_left[:basis, :basis], margin_to_up, with_right[:basis, :basis], blank], 1)
    part_out[3] = jnp.concatenate([with_left[basis:, basis:], margin_to_down, with_right[basis:, basis:], blank], 1)
    part_up = remote(PART_UP, part_out.at[2], part_in.at[2], up)
    part_down = remote(PART_DOWN, part_out.at[3], part_in.at[3], down)
    part_up.start()
    part_down.start()

    fold = lax.broadcasted_iota(jnp.int32, (basis, 2 * basis), 1) < basis
    rows_of_left = collapse(acc_v[1])
    part_out[1] = jnp.concatenate(
        [jnp.where(fold, pairs_t[0][:basis], pairs_t[0][basis:]), rows_of_left, blank], 1
    )
    part_l = remote(PART_L, part_out.at[1], part_in.at[1], left)
    part_l.start()
    rows_of_right = collapse(acc_v[2])
    part_out[0] = jnp.concatenate(
        [jnp.where(fold, pairs_t[1][:basis], pairs_t[1][basis:]), rows_of_right, blank], 1
    )
    part_r = remote(PART_R, part_out.at[0], part_in.at[0], right)
    part_r.start()

    part_up.wait_recv()
    part_down.wait_recv()
    part_l.wait_recv()
    part_r.wait_recv()
    west, east, below, above = part_in[0], part_in[1], part_in[2], part_in[3]

    def inside(condition, block):
        return jnp.where(jnp.full(block.shape, condition.astype(jnp.int32), jnp.int32) > 0, block, jnp.zeros_like(block))

    has_west, has_east, has_below, has_above = lat > 0, lat < lat_n - 1, dep > 0, dep < depth_n - 1
    lateral_ref[0, 0, 0] = inside(has_west, rows_of_left.T + west[:, 2 * basis : 3 * basis])
    lateral_ref[0, 0, 1] = own_block
    lateral_ref[0, 0, 2] = inside(has_east, rows_of_right.T + east[:, 2 * basis : 3 * basis])
    vertical_ref[0, 0, 0, 0] = inside(has_below & has_west, -(below[:, :basis] + west[:, basis : 2 * basis]))
    vertical_ref[0, 0, 0, 1] = inside(has_below, -(below[:, basis : 2 * basis] + across_down))
    vertical_ref[0, 0, 0, 2] = inside(
        has_below & has_east, -(below[:, 2 * basis : 3 * basis] + east[:, basis : 2 * basis])
    )
    vertical_ref[0, 0, 1, 0] = inside(has_above & has_west, -(above[:, :basis] + west[:, :basis]))
    vertical_ref[0, 0, 1, 1] = inside(has_above, -(above[:, basis : 2 * basis] + across_up))
    vertical_ref[0, 0, 1, 2] = inside(has_above & has_east, -(above[:, 2 * basis : 3 * basis] + east[:, :basis]))

    for copy in [
        strip_r, strip_l, edge_r, own_up, own_down, margin_up, margin_down, part_up, part_down, part_l, part_r,
        *bulk_r, *bulk_l,
    ]:
        copy.wait_send()


def body(lat_n, depth_n, own_basis, left_margin, right_margin, permeability, cluster_mask, intersection_width):
    basis, cells, layers, north = own_basis.shape
    margin = left_margin.shape[1]
    rows = basis * layers
    any_space = pl.BlockSpec(memory_space=pl.ANY)
    vmem = pl.BlockSpec(memory_space=pltpu.VMEM)
    scratch = [
        pltpu.VMEM(own_basis.shape, bf16),
        pltpu.VMEM(left_margin.shape, bf16),
        pltpu.VMEM(right_margin.shape, bf16),
        pltpu.VMEM(permeability.shape, f32),
        pltpu.VMEM(cluster_mask.shape, jnp.int32),
        pltpu.SMEM(intersection_width.shape, jnp.int32),
        pltpu.VMEM((cells, layers, north), f32),
        pltpu.VMEM((2, margin + 1, layers, north), bf16),
        pltpu.VMEM((2, margin + 1, layers, north), bf16),
        pltpu.VMEM((4, margin, layers, north), f32),
        pltpu.VMEM((rows, (cells + 2) * north), bf16),
        pltpu.VMEM((rows, cells * north), bf16),
        pltpu.VMEM((rows, cells * north), bf16),
        pltpu.VMEM((rows, north), bf16),
        pltpu.VMEM((2, rows, (margin + 1) * north), bf16),
        pltpu.VMEM((2, rows, margin * north), bf16),
        pltpu.VMEM((2, rows, margin * north), bf16),
        pltpu.VMEM((2, basis, margin, layers, north), bf16),
        pltpu.VMEM((2, rows, margin * north), bf16),
        pltpu.VMEM((2 * basis, cells * north), bf16),
        pltpu.VMEM((2 * basis, cells * north), bf16),
        pltpu.VMEM((2, 2 * basis, margin * north), bf16),
        pltpu.VMEM((2, basis, margin * north), bf16),
        pltpu.VMEM((3, rows, rows), f32),
        pltpu.VMEM((4, basis, 4 * basis), f32),
        pltpu.VMEM((4, basis, 4 * basis), f32),
        pltpu.SemaphoreType.DMA((6,)),
        pltpu.SemaphoreType.DMA((REMOTE,)),
        pltpu.SemaphoreType.DMA((REMOTE,)),
    ]
    return pl.pallas_call(
        functools.partial(kernel, lat_n, depth_n),
        out_shape=(
            jax.ShapeDtypeStruct((1, 1, 3, basis, basis), f32),
            jax.ShapeDtypeStruct((1, 1, 2, 3, basis, basis), f32),
        ),
        in_specs=[any_space] * 6,
        out_specs=(vmem, vmem),
        scratch_shapes=scratch,
        compiler_params=pltpu.CompilerParams(
            collective_id=0, has_side_effects=True, vmem_limit_bytes=56 * 1024 * 1024
        ),
    )(own_basis, left_margin, right_margin, permeability, cluster_mask, intersection_width)


def solution(mesh):
    in_specs = (
        P(None, "lat", "depth", None),
        P(None, "lat", "depth", None),
        P(None, "lat", "depth", None),
        P("lat", "depth", None),
        P("lat", "depth"),
        P("lat", "depth", None),
    )
    out_specs = (P("lat", "depth", None, None, None), P("lat", "depth", None, None, None, None))
    return jax.shard_map(
        functools.partial(body, mesh.shape["lat"], mesh.shape["depth"]),
        mesh=mesh, in_specs=in_specs, out_specs=out_specs, check_vma=False,
    )
```

time: 116 us -> 41.9 us (0.36)
  the two profiles are of different devices: /device:TPU:153 before, /device:TPU:1 now
where the time goes in v1:
time: 41.9 us; the launch traced here: 41.7 us
  Pallas kernels  36.7 us (88%)
  local copies, waits for them, and re-layouts  4.33 us (10%)
  between operations  0.64 us (2%)
    pallas_call x1, Pallas kernels, body(): pl.pallas_call(functools.partial(kernel, lat_n, depth_n), out_shape=(jax....  36.7 us
    unnamed x3, local copies, waits for them, and re-layouts  4.33 us

profile of v1, /device:TPU:1, one launch (start us, length us, event | category | flops | bytes accessed | tf_op | source)
XLA Modules:
  0.0 41.7 jit_solution(903500855995762775)
XLA Ops:
  0.6 1.4 %copy.8.mask_hbm = s32[40,8]{1,0:T(8,128)} copy(s32[40,8]{0,1:T(8,128)} %param.10) | data formatting | bytes 2560 | tf_op args[4]
  2.0 36.7 %shard_map.77 = (f32[1,1,3,32,32]{4,3,2,1,0:T(8,128)}, f32[1,1,2,3,32,32]{5,4,3,2,1,0:T(8,128)}) custom-call(bf16[32,40,8,128]{3,2,1,0:T(8,128)(2,1)} %own_hbm.1, bf16[32,16,8,128]{3,2,1,0:T(8,128)(2,1)} %left_hbm.1, bf16[32,16,8,128]{3,2,1,0:T(8,128)(2,1)} %right_hbm.1, f32[40,8,128]{2,1,0:T(8,128)} %perm_hbm.1, s32[40,8]{1,0:T(8,128)} %copy.8.mask_hbm, ...), custom_call_target="tpu_custom_call" | custom-call | tf_op jit(solution)/shard_map/pallas_call | solution.py:382
  38.7 1.4 %copy.11 = f32[1,1,3,32,32]{4,3,2,1,0:T(8,128)} copy(f32[1,1,3,32,32]{4,3,2,1,0:T(8,128)} %get-tuple-element.4) | data formatting | bytes 24576
  40.2 1.5 %copy.12 = f32[1,1,2,3,32,32]{5,4,3,2,1,0:T(8,128)} copy(f32[1,1,2,3,32,32]{5,4,3,2,1,0:T(8,128)} %get-tuple-element.5) | data formatting | bytes 49152

commit v2 on v1

v2 whole, which is shorter than its diff:
```python
import functools

import jax
import jax.numpy as jnp
from jax import lax
from jax.experimental import pallas as pl
from jax.experimental.pallas import tpu as pltpu
from jax.sharding import PartitionSpec as P

MESH = pl.DeviceIdType.MESH
f32 = jnp.float32
bf16 = jnp.bfloat16
diagonal_weight = 6.1

CHUNKS = (4, 4, 4, 4)

STRIP_R, STRIP_L, EDGE_R, OWN_UP, OWN_DOWN, MARGIN_UP, MARGIN_DOWN, PART_R, PART_L, PART_UP, PART_DOWN = range(11)
BULK_R = 11
BULK_L = BULK_R + len(CHUNKS)
REMOTE = BULK_L + len(CHUNKS)

PERM, MASK, WIDTH, LEFT, RIGHT, OWN = range(6)


def nt(left, right):
    return lax.dot_general(left, right, (((1,), (1,)), ((), ())), preferred_element_type=f32)


def nn(left, right):
    return jnp.dot(left, right, preferred_element_type=f32)


def split(value):
    high = value.astype(bf16)
    return high, (value - high.astype(f32)).astype(bf16)


def iota(shape, dim):
    return lax.broadcasted_iota(jnp.int32, shape, dim)


class Message:
    def __init__(self, copy, sends, receives):
        self.copy, self.sends, self.receives = copy, sends, receives

    def start(self):
        pl.when(self.sends)(self.copy.start)

    def wait_recv(self):
        pl.when(self.receives)(self.copy.wait_recv)

    def wait_send(self):
        pl.when(self.sends)(self.copy.wait_send)


def kernel(
    lat_n, depth_n,
    own_hbm, left_hbm, right_hbm, perm_hbm, mask_hbm, width_hbm,
    out_ref,
    own_v, left_v, right_v, perm_v, mask_v, width_s,
    scale_v, strip_out, strip_in, factor_v,
    field_v, high_v, low_v, north_v, edge_in,
    land_v, other_v,
    planes_v, mabove_v, stack_v,
    part_out, part_in,
    local_sem, send_sem, recv_sem,
):
    basis, cells, layers, north = own_hbm.shape
    margin = left_hbm.shape[1]
    rows = basis * layers
    lat, dep = lax.axis_index("lat"), lax.axis_index("depth")
    has_west, has_east, has_below, has_above = lat > 0, lat < lat_n - 1, dep > 0, dep < depth_n - 1
    right = (lax.rem(lat + 1, lat_n), dep)
    left = (lax.rem(lat + lat_n - 1, lat_n), dep)
    up = (lat, lax.rem(dep + 1, depth_n))
    down = (lat, lax.rem(dep + depth_n - 1, depth_n))
    ways = {
        "right": (right, has_east, has_west),
        "left": (left, has_west, has_east),
        "up": (up, has_above, has_below),
        "down": (down, has_below, has_above),
    }

    def remote(index, src, dst, way):
        device, sends, receives = ways[way]
        copy = pltpu.make_async_remote_copy(
            src_ref=src, dst_ref=dst, send_sem=send_sem.at[index], recv_sem=recv_sem.at[index],
            device_id=device, device_id_type=MESH,
        )
        return Message(copy, sends, receives)

    def columns(plane, count):
        return pl.ds(pl.multiple_of(plane * north, north), count * north)

    barrier = pltpu.get_barrier_semaphore()
    for device, exists, _ in ways.values():

        @pl.when(exists)
        def _(device=device):
            pl.semaphore_signal(barrier, inc=1, device_id=device, device_id_type=MESH)

    local = [
        pltpu.make_async_copy(perm_hbm, perm_v, local_sem.at[PERM]),
        pltpu.make_async_copy(mask_hbm, mask_v, local_sem.at[MASK]),
        pltpu.make_async_copy(width_hbm, width_s, local_sem.at[WIDTH]),
        pltpu.make_async_copy(left_hbm, left_v, local_sem.at[LEFT]),
        pltpu.make_async_copy(right_hbm, right_v, local_sem.at[RIGHT]),
        pltpu.make_async_copy(own_hbm, own_v, local_sem.at[OWN]),
    ]
    for index in (PERM, MASK, WIDTH, OWN, LEFT, RIGHT):
        local[index].start()
    for index in (PERM, MASK, WIDTH):
        local[index].wait()

    factor = 0.05 + 0.95 * mask_v[...].astype(f32)
    for cell in range(cells):
        wide = jnp.broadcast_to(factor[:, cell : cell + 1], (layers, north))
        scale_v[cell] = jnp.sqrt(perm_v[cell] * wide).astype(bf16).astype(f32)
    left_width, right_width = width_s[0, 0, 0], width_s[0, 0, 1]
    strip_out[0, 0:margin] = scale_v[cells - margin : cells].astype(bf16)
    strip_out[0, margin] = jnp.full((layers, north), right_width.astype(f32), f32).astype(bf16)
    strip_out[1, 0:margin] = scale_v[0:margin].astype(bf16)
    strip_out[1, margin] = jnp.full((layers, north), left_width.astype(f32), f32).astype(bf16)

    peers = (
        lax.div(lat + lat_n - 1, lat_n) + lax.div(2 * lat_n - 2 - lat, lat_n)
        + lax.div(dep + depth_n - 1, depth_n) + lax.div(2 * depth_n - 2 - dep, depth_n)
    )
    pl.semaphore_wait(barrier, peers)
    strip_r = remote(STRIP_R, strip_out.at[0], strip_in.at[0], "right")
    strip_l = remote(STRIP_L, strip_out.at[1], strip_in.at[1], "left")
    strip_r.start()
    strip_l.start()
    bulk_r, bulk_l, begins = [], [], []
    begin = 0
    for c, size in enumerate(CHUNKS):
        part = pl.ds(begin, size)
        bulk_r.append(remote(BULK_R + c, right_hbm.at[:, part], land_v.at[0, :, part], "right"))
        bulk_l.append(remote(BULK_L + c, left_hbm.at[:, part], land_v.at[1, :, part], "left"))
        bulk_r[c].start()
        bulk_l[c].start()
        begins.append(begin)
        begin += size

    pick_row = iota((2 * basis, rows), 0)
    wanted = jnp.where(pick_row < basis, pick_row * layers + layers - 1, (pick_row - basis) * layers)
    pick = (iota((2 * basis, rows), 1) == wanted).astype(f32).astype(bf16)

    first_own = margin + 1
    first_right = first_own + cells + 1
    for plane in (margin, first_right - 1, first_right + margin):
        field_v[:, plane * north : (plane + 1) * north] = jnp.zeros((rows, north), bf16)

    pair = 2 * north
    r, c = iota((pair, pair), 0), iota((pair, pair), 1)
    next_north = ((r - c == 1) & (r // north == c // north)).astype(f32).astype(bf16)
    in_pair = (((jnp.abs(r - c) == 1) & (r // north == c // north)) | (jnp.abs(r - c) == north)).astype(f32).astype(bf16)
    r, c = iota((rows, rows), 0), iota((rows, rows), 1)
    depth_sum = ((jnp.abs(r - c) == 1) & (r // layers == c // layers)).astype(f32).astype(bf16)

    def scaled(values, factors):
        return (values.astype(f32) * factors[None]).reshape(rows, north).astype(bf16)

    def fill(source, factors, first, count, group, side=None):
        def step(index, carry):
            base = index * group
            for j in range(group):
                field_v[:, columns(first + base + j, 1)] = scaled(source[:, base + j], factors(base + j))
            planes_v[:, columns(first + base, group)] = nn(
                pick, field_v[:, columns(first + base, group)]
            ).astype(bf16)
            if side is not None:
                for j in range(0, group, 2):
                    north_v[side, :, columns(base + j, 2)] = nn(
                        field_v[:, columns(first + base + j, 2)], next_north
                    ).astype(bf16)
            return carry

        lax.fori_loop(0, count // group, step, 0)

    local[OWN].wait()
    fill(own_v, lambda plane: scale_v[plane], first_own, cells, 8)
    own_columns = pl.ds(first_own * north, cells * north)
    own_up = remote(OWN_UP, planes_v.at[0:basis, own_columns], stack_v.at[basis : 2 * basis], "up")
    own_down = remote(OWN_DOWN, planes_v.at[basis : 2 * basis, own_columns], stack_v.at[0:basis], "down")
    own_up.start()
    own_down.start()
    edge_r = remote(EDGE_R, field_v.at[:, pl.ds((first_right - 2) * north, north)], edge_in, "right")
    edge_r.start()

    strip_r.wait_recv()
    strip_l.wait_recv()
    at = iota((margin, layers, north), 0).astype(f32)
    none = jnp.zeros((margin, layers, north), f32)
    from_left = strip_in[0].astype(f32)
    from_right = strip_in[1].astype(f32)
    factor_v[0] = jnp.where(at >= margin - left_width.astype(f32), from_left[:margin], none)
    factor_v[1] = jnp.where(at < right_width.astype(f32), from_right[:margin], none)
    factor_v[2] = jnp.where(at < from_left[margin:], scale_v[0:margin], none)
    factor_v[3] = jnp.where(at >= margin - from_right[margin:], scale_v[cells - margin : cells], none)
    local[LEFT].wait()
    local[RIGHT].wait()
    fill(left_v, lambda plane: factor_v[0, plane], 0, margin, 8, 0)
    fill(right_v, lambda plane: factor_v[1, plane], first_right, margin, 8, 1)
    margin_columns = (pl.ds(0, margin * north), pl.ds(first_right * north, margin * north))
    margin_up = remote(MARGIN_UP, planes_v.at[0:basis, margin_columns[0]], mabove_v.at[0], "up")
    margin_down = remote(
        MARGIN_DOWN, planes_v.at[basis : 2 * basis, margin_columns[1]], mabove_v.at[1], "down"
    )
    margin_up.start()
    margin_down.start()

    def operator(step, carry):
        for part in range(0, 8, 2):
            cell = step * 8 + part
            both = field_v[:, columns(first_own + cell, 2)]
            sums = nn(jnp.concatenate([both, depth_sum], 1), jnp.concatenate([in_pair, both], 0))
            for j, outer in ((0, -1), (1, 2)):
                middle = both[:, j * north : (j + 1) * north].astype(f32)
                beside = field_v[:, columns(first_own + cell + outer, 1)].astype(f32)
                value = diagonal_weight * middle - sums[:, j * north : (j + 1) * north] - beside
                high, low = split(value)
                high_v[:, columns(cell + j, 1)] = high
                low_v[:, columns(cell + j, 1)] = low
        return carry

    lax.fori_loop(0, cells // 8, operator, 0)

    r_layer, c_layer = lax.rem(r, layers), lax.rem(c, layers)
    same_layer = r_layer == c_layer
    half_weight = jnp.where(same_layer, 0.5 * diagonal_weight, jnp.where(c_layer - r_layer == 1, -1.0, 0.0))
    gather = (iota((rows, basis), 0) // layers == iota((rows, basis), 1)).astype(f32)

    def gathered(kept):
        summed = jnp.sum(kept.reshape(basis, layers, rows), axis=1)
        return jnp.dot(summed, gather, precision=lax.Precision.HIGHEST, preferred_element_type=f32)

    def collapse(matrix):
        return gathered(jnp.where(same_layer, matrix, jnp.zeros_like(matrix)))

    own_fields = field_v[:, first_own * north : (first_own + cells) * north]
    own_sum = nt(own_fields, high_v[...]) + nt(own_fields, low_v[...])
    squares, steps = [], []
    for side, first in ((0, 0), (1, first_right)):
        fields = field_v[:, first * north : (first + margin) * north]
        squares.append(nt(fields, fields))
        steps.append(nt(fields, field_v[:, (first + 1) * north : (first + margin + 1) * north]) + nt(fields, north_v[side]))

    def plane_of(plane):
        return field_v[:, plane * north : (plane + 1) * north]

    border = nt(
        jnp.concatenate([plane_of(margin - 1), plane_of(first_right - 2)], 1),
        jnp.concatenate([plane_of(first_own), plane_of(first_right)], 1),
    )
    own_block = gathered(
        half_weight * (squares[0] + squares[1])
        + jnp.where(same_layer, 0.5 * own_sum - (steps[0] + steps[1] + border), jnp.zeros_like(own_sum))
    )
    out_ref[1] = own_block + own_block.T

    own_up.wait_recv()
    own_down.wait_recv()
    across = nt(planes_v[:, first_own * north : (first_own + cells) * north], stack_v[0 : 2 * basis])
    margin_up.wait_recv()
    margin_down.wait_recv()
    left_bottom = planes_v[basis : 2 * basis, margin_columns[0]]
    right_top = planes_v[0:basis, margin_columns[1]]
    across_down = across[basis:, basis:] + nt(left_bottom, mabove_v[0])
    across_up = across[:basis, :basis] + nt(right_top, mabove_v[1])
    margin_to_down = nt(mabove_v[0], left_bottom)
    margin_to_up = nt(mabove_v[1], right_top)

    edge_r.wait_recv()
    starts = (0, cells - margin)
    totals = [None, None]
    for c, size in enumerate(CHUNKS):
        for side, bulk in ((0, bulk_r), (1, bulk_l)):
            bulk[c].wait_recv()
            for plane in range(begins[c], begins[c] + size):
                other_v[side, :, plane * north : (plane + 1) * north] = scaled(
                    land_v[side, :, plane], factor_v[2 + side, plane]
                )
            other = other_v[side, :, begins[c] * north : (begins[c] + size) * north]
            at_own = pl.ds((starts[side] + begins[c]) * north, size * north)
            term = nt(other, high_v[:, at_own]) + nt(other, low_v[:, at_own])
            if side == 0 and c == 0:
                far = jnp.concatenate([edge_in[...], other[:, :north]], 1)
                near = -jnp.concatenate([plane_of(first_own), plane_of(margin - 1)], 1)
                term = term + nt(far, near)
            totals[side] = term if c == 0 else totals[side] + term
            stack_v[2 * basis : 4 * basis, at_own] = nn(pick, other).astype(bf16)

    pairs = []
    for side in range(2):
        stack = stack_v[:, starts[side] * north : (starts[side] + margin) * north]
        pairs.append(nt(stack, stack))
    with_left, with_right = (both[: 2 * basis, 2 * basis :] for both in pairs)
    blank = jnp.zeros((basis, basis), f32)
    part_out[2] = jnp.concatenate([with_left[:basis, :basis], margin_to_up, with_right[:basis, :basis], blank], 1)
    part_out[3] = jnp.concatenate([with_left[basis:, basis:], margin_to_down, with_right[basis:, basis:], blank], 1)
    part_up = remote(PART_UP, part_out.at[2], part_in.at[2], "up")
    part_down = remote(PART_DOWN, part_out.at[3], part_in.at[3], "down")
    part_up.start()
    part_down.start()

    fold = iota((basis, 2 * basis), 1) < basis
    turned = [
        jnp.where(fold, both[2 * basis : 3 * basis, : 2 * basis], both[3 * basis :, : 2 * basis]) for both in pairs
    ]
    rows_of_left = collapse(totals[0])
    part_out[1] = jnp.concatenate([turned[0], rows_of_left, blank], 1)
    part_l = remote(PART_L, part_out.at[1], part_in.at[1], "left")
    part_l.start()
    rows_of_right = collapse(totals[1])
    part_out[0] = jnp.concatenate([turned[1], rows_of_right, blank], 1)
    part_r = remote(PART_R, part_out.at[0], part_in.at[0], "right")
    part_r.start()

    part_up.wait_recv()
    part_down.wait_recv()
    part_l.wait_recv()
    part_r.wait_recv()
    west, east, below, above = part_in[0], part_in[1], part_in[2], part_in[3]

    def inside(condition, block):
        return jnp.where(jnp.full(block.shape, condition.astype(jnp.int32), jnp.int32) > 0, block, jnp.zeros_like(block))

    out_ref[0] = inside(has_west, rows_of_left.T + west[:, 2 * basis : 3 * basis])
    out_ref[2] = inside(has_east, rows_of_right.T + east[:, 2 * basis : 3 * basis])
    out_ref[3] = inside(has_below & has_west, -(below[:, :basis] + west[:, basis : 2 * basis]))
    out_ref[4] = inside(has_below, -(below[:, basis : 2 * basis] + across_down))
    out_ref[5] = inside(has_below & has_east, -(below[:, 2 * basis : 3 * basis] + east[:, basis : 2 * basis]))
    out_ref[6] = inside(has_above & has_west, -(above[:, :basis] + west[:, :basis]))
    out_ref[7] = inside(has_above, -(above[:, basis : 2 * basis] + across_up))
    out_ref[8] = inside(has_above & has_east, -(above[:, 2 * basis : 3 * basis] + east[:, :basis]))

    for copy in [
        strip_r, strip_l, edge_r, own_up, own_down, margin_up, margin_down, part_up, part_down, part_l, part_r,
        *bulk_r, *bulk_l,
    ]:
        copy.wait_send()


def hand_out(blocks_ref, lateral_ref, vertical_ref, sems):
    copies = [
        pltpu.make_async_copy(blocks_ref.at[0:3], lateral_ref.at[0, 0], sems.at[0]),
        pltpu.make_async_copy(blocks_ref.at[3:6], vertical_ref.at[0, 0, 0], sems.at[1]),
        pltpu.make_async_copy(blocks_ref.at[6:9], vertical_ref.at[0, 0, 1], sems.at[2]),
    ]
    for copy in copies:
        copy.start()
    for copy in copies:
        copy.wait()


def body(lat_n, depth_n, own_basis, left_margin, right_margin, permeability, cluster_mask, intersection_width):
    basis, cells, layers, north = own_basis.shape
    margin = left_margin.shape[1]
    rows = basis * layers
    planes = cells + 2 * margin + 3
    any_space = pl.BlockSpec(memory_space=pl.ANY)
    vmem = pl.BlockSpec(memory_space=pltpu.VMEM)
    scratch = [
        pltpu.VMEM(own_basis.shape, bf16),
        pltpu.VMEM(left_margin.shape, bf16),
        pltpu.VMEM(right_margin.shape, bf16),
        pltpu.VMEM(permeability.shape, f32),
        pltpu.VMEM((layers, cells), jnp.int32),
        pltpu.SMEM(intersection_width.shape, jnp.int32),
        pltpu.VMEM((cells, layers, north), f32),
        pltpu.VMEM((2, margin + 1, layers, north), bf16),
        pltpu.VMEM((2, margin + 1, layers, north), bf16),
        pltpu.VMEM((4, margin, layers, north), f32),
        pltpu.VMEM((rows, planes * north), bf16),
        pltpu.VMEM((rows, cells * north), bf16),
        pltpu.VMEM((rows, cells * north), bf16),
        pltpu.VMEM((2, rows, margin * north), bf16),
        pltpu.VMEM((rows, north), bf16),
        pltpu.VMEM((2, basis, margin, layers, north), bf16),
        pltpu.VMEM((2, rows, margin * north), bf16),
        pltpu.VMEM((2 * basis, planes * north), bf16),
        pltpu.VMEM((2, basis, margin * north), bf16),
        pltpu.VMEM((4 * basis, cells * north), bf16),
        pltpu.VMEM((4, basis, 4 * basis), f32),
        pltpu.VMEM((4, basis, 4 * basis), f32),
        pltpu.SemaphoreType.DMA((6,)),
        pltpu.SemaphoreType.DMA((REMOTE,)),
        pltpu.SemaphoreType.DMA((REMOTE,)),
    ]
    blocks = pl.pallas_call(
        functools.partial(kernel, lat_n, depth_n),
        out_shape=jax.ShapeDtypeStruct((9, basis, basis), f32),
        in_specs=[any_space] * 6,
        out_specs=vmem,
        scratch_shapes=scratch,
        compiler_params=pltpu.CompilerParams(
            collective_id=0, has_side_effects=True, vmem_limit_bytes=56 * 1024 * 1024
        ),
    )(own_basis, left_margin, right_margin, permeability, cluster_mask.T, intersection_width)
    return pl.pallas_call(
        hand_out,
        out_shape=(
            jax.ShapeDtypeStruct((1, 1, 3, basis, basis), f32),
            jax.ShapeDtypeStruct((1, 1, 2, 3, basis, basis), f32),
        ),
        in_specs=[vmem],
        out_specs=(any_space, any_space),
        scratch_shapes=[pltpu.SemaphoreType.DMA((3,))],
    )(blocks)


def solution(mesh):
    in_specs = (
        P(None, "lat", "depth", None),
        P(None, "lat", "depth", None),
        P(None, "lat", "depth", None),
        P("lat", "depth", None),
        P("lat", "depth"),
        P("lat", "depth", None),
    )
    out_specs = (P("lat", "depth", None, None, None), P("lat", "depth", None, None, None, None))
    return jax.shard_map(
        functools.partial(body, mesh.shape["lat"], mesh.shape["depth"]),
        mesh=mesh, in_specs=in_specs, out_specs=out_specs, check_vma=False,
    )
```

time: 41.9 us -> 30.3 us (0.72)
  the two profiles are of different devices: /device:TPU:1 before, /device:TPU:70 now
where the time goes in v2:
time: 30.3 us; the launch traced here: 30.2 us
  Pallas kernels  29.6 us (98%)
  between operations  0.64 us (2%)
    pallas_call x1, Pallas kernels, body(): pl.pallas_call(functools.partial(kernel, lat_n, depth_n), out_shape=jax.S...  28 us
    pallas_call x1, Pallas kernels, body(): pl.pallas_call(hand_out, out_shape=(jax.ShapeDtypeStruct((1, 1, 3, basis,...  1.59 us

profile of v2, /device:TPU:70, one launch (start us, length us, event | category | flops | bytes accessed | tf_op | source)
XLA Modules:
  0.0 30.2 jit_solution(12494115759853164172)
XLA Ops:
  0.6 28.0 %shard_map.77.blocks_ref = f32[9,32,32]{2,1,0:T(8,128)} custom-call(bf16[32,40,8,128]{3,2,1,0:T(8,128)(2,1)} %own_hbm.1, bf16[32,16,8,128]{3,2,1,0:T(8,128)(2,1)} %left_hbm.1, bf16[32,16,8,128]{3,2,1,0:T(8,128)(2,1)} %right_hbm.1, f32[40,8,128]{2,1,0:T(8,128)} %perm_hbm.1, s32[8,40]{1,0:T(8,128)} %bitcast.1, s32[1,1,2]{2,1,0:T(1,128)} %width_hbm.1), custom_call_target="tpu_custom_call" | custom-call | tf_op jit(solution)/shard_map/pallas_call | solution.py:391
  28.6 1.6 %shard_map.78 = (f32[1,1,3,32,32]{4,3,2,1,0:T(8,128)}, f32[1,1,2,3,32,32]{5,4,3,2,1,0:T(8,128)}) custom-call(f32[9,32,32]{2,1,0:T(8,128)} %shard_map.77.blocks_ref), custom_call_target="tpu_custom_call" | custom-call | tf_op jit(solution)/shard_map/pallas_call | solution.py:401

commit v3 on v2

--- a/solution.py
+++ b/solution.py
@@ -12,10 +12,13 @@
 bf16 = jnp.bfloat16
 diagonal_weight = 6.1
 
-CHUNKS = (4, 4, 4, 4)
-
-STRIP_R, STRIP_L, EDGE_R, OWN_UP, OWN_DOWN, MARGIN_UP, MARGIN_DOWN, PART_R, PART_L, PART_UP, PART_DOWN = range(11)
-BULK_R = 11
+CHUNKS = (8, 6, 2)
+
+STRIP_R, STRIP_L, EDGE_R, MARGIN_UP, MARGIN_DOWN, PART_R, PART_L, PART_UP, PART_DOWN = range(9)
+OWN_PARTS = (16, 24)
+OWN_UP = 9
+OWN_DOWN = OWN_UP + len(OWN_PARTS)
+BULK_R = OWN_DOWN + len(OWN_PARTS)
 BULK_L = BULK_R + len(CHUNKS)
 REMOTE = BULK_L + len(CHUNKS)
 
@@ -33,6 +36,11 @@
 def split(value):
     high = value.astype(bf16)
     return high, (value - high.astype(f32)).astype(bf16)
+
+
+def split_rest(value):
+    high = value.astype(bf16)
+    return high, value - high.astype(f32)
 
 
 def iota(shape, dim):
@@ -59,6 +67,7 @@
     out_ref,
     own_v, left_v, right_v, perm_v, mask_v, width_s,
     scale_v, strip_out, strip_in, factor_v,
+    pick_v, shift_v, weight_v, gather_v,
     field_v, high_v, low_v, north_v, edge_in,
     land_v, other_v,
     planes_v, mabove_v, stack_v,
@@ -109,6 +118,29 @@
     ]
     for index in (PERM, MASK, WIDTH, OWN, LEFT, RIGHT):
         local[index].start()
+    low_layer = layers.bit_length() - 1
+    pick_row, pick_col = iota((2 * basis, rows), 0), iota((2 * basis, rows), 1)
+    wanted = jnp.where(pick_row < basis, pick_row * layers + layers - 1, (pick_row - basis) * layers)
+    pick_v[...] = (pick_col == wanted).astype(f32).astype(bf16)
+    pair = 2 * north
+    r, c = iota((pair, pair), 0), iota((pair, pair), 1)
+    plane_bit = north.bit_length() - 1
+    one_plane = (r >> plane_bit) == (c >> plane_bit)
+    gap = r - c
+    shift_v[0] = jnp.where((gap == 1) & one_plane, 1.0, 0.0).astype(bf16)
+    beside = (jnp.abs(gap) == 1) & one_plane
+    shift_v[1] = jnp.where(beside | (jnp.abs(gap) == north), 1.0, 0.0).astype(bf16)
+    r, c = iota((rows, rows), 0), iota((rows, rows), 1)
+    gap = r - c
+    one_field = (r >> low_layer) == (c >> low_layer)
+    shift_v[2] = jnp.where((jnp.abs(gap) == 1) & one_field, 1.0, 0.0).astype(bf16)
+    r_layer, c_layer = r & (layers - 1), c & (layers - 1)
+    same = r_layer == c_layer
+    weight_v[0] = jnp.where(same, 1.0, 0.0)
+    weight_v[1] = jnp.where(same, 0.5 * diagonal_weight, jnp.where(c_layer - r_layer == 1, -1.0, 0.0))
+    r, c = iota((rows, basis), 0), iota((rows, basis), 1)
+    gather_v[...] = jnp.where((r >> low_layer) == c, 1.0, 0.0).astype(bf16)
+
     for index in (PERM, MASK, WIDTH):
         local[index].wait()
 
@@ -139,54 +171,66 @@
         bulk_l.append(remote(BULK_L + c, left_hbm.at[:, part], land_v.at[1, :, part], "left"))
         bulk_r[c].start()
         bulk_l[c].start()
+        if c == 0:
+            edge_r = remote(EDGE_R, own_hbm.at[:, pl.ds(cells - 1, 1)], edge_in, "right")
+            edge_r.start()
         begins.append(begin)
         begin += size
-
-    pick_row = iota((2 * basis, rows), 0)
-    wanted = jnp.where(pick_row < basis, pick_row * layers + layers - 1, (pick_row - basis) * layers)
-    pick = (iota((2 * basis, rows), 1) == wanted).astype(f32).astype(bf16)
 
     first_own = margin + 1
     first_right = first_own + cells + 1
     for plane in (margin, first_right - 1, first_right + margin):
         field_v[:, plane * north : (plane + 1) * north] = jnp.zeros((rows, north), bf16)
 
-    pair = 2 * north
-    r, c = iota((pair, pair), 0), iota((pair, pair), 1)
-    next_north = ((r - c == 1) & (r // north == c // north)).astype(f32).astype(bf16)
-    in_pair = (((jnp.abs(r - c) == 1) & (r // north == c // north)) | (jnp.abs(r - c) == north)).astype(f32).astype(bf16)
-    r, c = iota((rows, rows), 0), iota((rows, rows), 1)
-    depth_sum = ((jnp.abs(r - c) == 1) & (r // layers == c // layers)).astype(f32).astype(bf16)
-
     def scaled(values, factors):
         return (values.astype(f32) * factors[None]).reshape(rows, north).astype(bf16)
 
-    def fill(source, factors, first, count, group, side=None):
+    def fill(source, factors, first, count, group, side=None, begin=0):
         def step(index, carry):
-            base = index * group
+            base = begin + index * group
             for j in range(group):
                 field_v[:, columns(first + base + j, 1)] = scaled(source[:, base + j], factors(base + j))
             planes_v[:, columns(first + base, group)] = nn(
-                pick, field_v[:, columns(first + base, group)]
+                pick_v[...], field_v[:, columns(first + base, group)]
             ).astype(bf16)
             if side is not None:
                 for j in range(0, group, 2):
                     north_v[side, :, columns(base + j, 2)] = nn(
-                        field_v[:, columns(first + base + j, 2)], next_north
+                        field_v[:, columns(first + base + j, 2)], shift_v[0]
                     ).astype(bf16)
             return carry
 
         lax.fori_loop(0, count // group, step, 0)
 
     local[OWN].wait()
-    fill(own_v, lambda plane: scale_v[plane], first_own, cells, 8)
-    own_columns = pl.ds(first_own * north, cells * north)
-    own_up = remote(OWN_UP, planes_v.at[0:basis, own_columns], stack_v.at[basis : 2 * basis], "up")
-    own_down = remote(OWN_DOWN, planes_v.at[basis : 2 * basis, own_columns], stack_v.at[0:basis], "down")
-    own_up.start()
-    own_down.start()
-    edge_r = remote(EDGE_R, field_v.at[:, pl.ds((first_right - 2) * north, north)], edge_in, "right")
-    edge_r.start()
+    own_up, own_down = [], []
+    begin = 0
+    for part, size in enumerate(OWN_PARTS):
+        fill(own_v, lambda plane: scale_v[plane], first_own, size, 8, None, begin)
+        source, target = (pl.ds((first + begin) * north, size * north) for first in (first_own, 0))
+        own_up.append(remote(OWN_UP + part, planes_v.at[0:basis, source], stack_v.at[basis : 2 * basis, target], "up"))
+        own_down.append(
+            remote(OWN_DOWN + part, planes_v.at[basis : 2 * basis, source], stack_v.at[0:basis, target], "down")
+        )
+        own_up[part].start()
+        own_down[part].start()
+        begin += size
+
+    def operator(step, carry):
+        for part in range(0, 8, 2):
+            cell = step * 8 + part
+            both = field_v[:, columns(first_own + cell, 2)]
+            sums = nn(jnp.concatenate([both, shift_v[2]], 1), jnp.concatenate([shift_v[1], both], 0))
+            for j, outer in ((0, -1), (1, 2)):
+                middle = both[:, j * north : (j + 1) * north].astype(f32)
+                beside = field_v[:, columns(first_own + cell + outer, 1)].astype(f32)
+                value = diagonal_weight * middle - sums[:, j * north : (j + 1) * north] - beside
+                high, low = split(value)
+                high_v[:, columns(cell + j, 1)] = high
+                low_v[:, columns(cell + j, 1)] = low
+        return carry
+
+    lax.fori_loop(0, cells // 8, operator, 0)
 
     strip_r.wait_recv()
     strip_l.wait_recv()
@@ -210,33 +254,14 @@
     margin_up.start()
     margin_down.start()
 
-    def operator(step, carry):
-        for part in range(0, 8, 2):
-            cell = step * 8 + part
-            both = field_v[:, columns(first_own + cell, 2)]
-            sums = nn(jnp.concatenate([both, depth_sum], 1), jnp.concatenate([in_pair, both], 0))
-            for j, outer in ((0, -1), (1, 2)):
-                middle = both[:, j * north : (j + 1) * north].astype(f32)
-                beside = field_v[:, columns(first_own + cell + outer, 1)].astype(f32)
-                value = diagonal_weight * middle - sums[:, j * north : (j + 1) * north] - beside
-                high, low = split(value)
-                high_v[:, columns(cell + j, 1)] = high
-                low_v[:, columns(cell + j, 1)] = low
-        return carry
-
-    lax.fori_loop(0, cells // 8, operator, 0)
-
-    r_layer, c_layer = lax.rem(r, layers), lax.rem(c, layers)
-    same_layer = r_layer == c_layer
-    half_weight = jnp.where(same_layer, 0.5 * diagonal_weight, jnp.where(c_layer - r_layer == 1, -1.0, 0.0))
-    gather = (iota((rows, basis), 0) // layers == iota((rows, basis), 1)).astype(f32)
-
-    def gathered(kept):
-        summed = jnp.sum(kept.reshape(basis, layers, rows), axis=1)
-        return jnp.dot(summed, gather, precision=lax.Precision.HIGHEST, preferred_element_type=f32)
-
-    def collapse(matrix):
-        return gathered(jnp.where(same_layer, matrix, jnp.zeros_like(matrix)))
+    def gathered(*kept):
+        summed = jnp.concatenate([jnp.sum(each.reshape(basis, layers, rows), axis=1) for each in kept], 0)
+        high, rest = split_rest(summed)
+        middle, rest = split_rest(rest)
+        return nn(
+            jnp.concatenate([high, middle, rest.astype(bf16)], 1),
+            jnp.concatenate([gather_v[...], gather_v[...], gather_v[...]], 0),
+        )
 
     own_fields = field_v[:, first_own * north : (first_own + cells) * north]
     own_sum = nt(own_fields, high_v[...]) + nt(own_fields, low_v[...])
@@ -254,14 +279,49 @@
         jnp.concatenate([plane_of(first_own), plane_of(first_right)], 1),
     )
     own_block = gathered(
-        half_weight * (squares[0] + squares[1])
-        + jnp.where(same_layer, 0.5 * own_sum - (steps[0] + steps[1] + border), jnp.zeros_like(own_sum))
+        weight_v[1] * (squares[0] + squares[1]) + weight_v[0] * (0.5 * own_sum - (steps[0] + steps[1] + border))
     )
     out_ref[1] = own_block + own_block.T
 
-    own_up.wait_recv()
-    own_down.wait_recv()
+    starts = (0, cells - margin)
+    totals, pairs = [None, None], [None, None]
+
+    def receive(c):
+        bulk_r[c].wait_recv()
+        bulk_l[c].wait_recv()
+        first, size = begins[c], CHUNKS[c]
+        part = slice(first * north, (first + size) * north)
+        for side in range(2):
+            for plane in range(first, first + size):
+                other_v[side, :, plane * north : (plane + 1) * north] = scaled(
+                    land_v[side, :, plane], factor_v[2 + side, plane]
+                )
+        for side in range(2):
+            other = other_v[side, :, part]
+            at_own = slice((starts[side] + first) * north, (starts[side] + first + size) * north)
+            term = nt(other, high_v[:, at_own]) + nt(other, low_v[:, at_own])
+            totals[side] = term if c == 0 else totals[side] + term
+            stack_v[2 * basis : 4 * basis, at_own] = nn(pick_v[...], other).astype(bf16)
+
+    def meet(first, size):
+        for side in range(2):
+            at_own = slice((starts[side] + first) * north, (starts[side] + first + size) * north)
+            stack = stack_v[:, at_own]
+            term = nt(stack, stack)
+            pairs[side] = term if pairs[side] is None else pairs[side] + term
+
+    receive(0)
+    for copy in (*own_up, *own_down):
+        copy.wait_recv()
     across = nt(planes_v[:, first_own * north : (first_own + cells) * north], stack_v[0 : 2 * basis])
+    for c in range(1, len(CHUNKS) - 1):
+        receive(c)
+    edge_r.wait_recv()
+    edge = scaled(edge_in[:, 0], strip_in[0, margin - 1].astype(f32))
+    far = jnp.concatenate([edge, other_v[0, :, 0:north]], 1)
+    near = -jnp.concatenate([plane_of(first_own), plane_of(margin - 1)], 1)
+    totals[0] = totals[0] + nt(far, near)
+    meet(0, begins[-1])
     margin_up.wait_recv()
     margin_down.wait_recv()
     left_bottom = planes_v[basis : 2 * basis, margin_columns[0]]
@@ -270,75 +330,54 @@
     across_up = across[:basis, :basis] + nt(right_top, mabove_v[1])
     margin_to_down = nt(mabove_v[0], left_bottom)
     margin_to_up = nt(mabove_v[1], right_top)
-
-    edge_r.wait_recv()
-    starts = (0, cells - margin)
-    totals = [None, None]
-    for c, size in enumerate(CHUNKS):
-        for side, bulk in ((0, bulk_r), (1, bulk_l)):
-            bulk[c].wait_recv()
-            for plane in range(begins[c], begins[c] + size):
-                other_v[side, :, plane * north : (plane + 1) * north] = scaled(
-                    land_v[side, :, plane], factor_v[2 + side, plane]
-                )
-            other = other_v[side, :, begins[c] * north : (begins[c] + size) * north]
-            at_own = pl.ds((starts[side] + begins[c]) * north, size * north)
-            term = nt(other, high_v[:, at_own]) + nt(other, low_v[:, at_own])
-            if side == 0 and c == 0:
-                far = jnp.concatenate([edge_in[...], other[:, :north]], 1)
-                near = -jnp.concatenate([plane_of(first_own), plane_of(margin - 1)], 1)
-                term = term + nt(far, near)
-            totals[side] = term if c == 0 else totals[side] + term
-            stack_v[2 * basis : 4 * basis, at_own] = nn(pick, other).astype(bf16)
-
-    pairs = []
-    for side in range(2):
-        stack = stack_v[:, starts[side] * north : (starts[side] + margin) * north]
-        pairs.append(nt(stack, stack))
+    receive(len(CHUNKS) - 1)
+    meet(begins[-1], CHUNKS[-1])
+
     with_left, with_right = (both[: 2 * basis, 2 * basis :] for both in pairs)
     blank = jnp.zeros((basis, basis), f32)
     part_out[2] = jnp.concatenate([with_left[:basis, :basis], margin_to_up, with_right[:basis, :basis], blank], 1)
     part_out[3] = jnp.concatenate([with_left[basis:, basis:], margin_to_down, with_right[basis:, basis:], blank], 1)
-    part_up = remote(PART_UP, part_out.at[2], part_in.at[2], "up")
-    part_down = remote(PART_DOWN, part_out.at[3], part_in.at[3], "down")
-    part_up.start()
-    part_down.start()
-
     fold = iota((basis, 2 * basis), 1) < basis
     turned = [
         jnp.where(fold, both[2 * basis : 3 * basis, : 2 * basis], both[3 * basis :, : 2 * basis]) for both in pairs
     ]
-    rows_of_left = collapse(totals[0])
+    both_rows = gathered(weight_v[0] * totals[0], weight_v[0] * totals[1])
+    rows_of_left, rows_of_right = both_rows[:basis], both_rows[basis:]
     part_out[1] = jnp.concatenate([turned[0], rows_of_left, blank], 1)
-    part_l = remote(PART_L, part_out.at[1], part_in.at[1], "left")
-    part_l.start()
-    rows_of_right = collapse(totals[1])
     part_out[0] = jnp.concatenate([turned[1], rows_of_right, blank], 1)
-    part_r = remote(PART_R, part_out.at[0], part_in.at[0], "right")
-    part_r.start()
-
-    part_up.wait_recv()
-    part_down.wait_recv()
-    part_l.wait_recv()
-    part_r.wait_recv()
+    parts = [
+        remote(PART_R, part_out.at[0], part_in.at[0], "right"),
+        remote(PART_L, part_out.at[1], part_in.at[1], "left"),
+        remote(PART_UP, part_out.at[2], part_in.at[2], "up"),
+        remote(PART_DOWN, part_out.at[3], part_in.at[3], "down"),
+    ]
+    for copy in parts:
+        copy.start()
+
+    out_ref[0] = rows_of_left.T
+    out_ref[2] = rows_of_right.T
+    out_ref[4] = across_down
+    out_ref[7] = across_up
+    for copy in [
+        strip_r, strip_l, edge_r, *own_up, *own_down, margin_up, margin_down, *bulk_r, *bulk_l,
+    ]:
+        copy.wait_send()
+    for copy in parts:
+        copy.wait_recv()
     west, east, below, above = part_in[0], part_in[1], part_in[2], part_in[3]
 
     def inside(condition, block):
         return jnp.where(jnp.full(block.shape, condition.astype(jnp.int32), jnp.int32) > 0, block, jnp.zeros_like(block))
 
-    out_ref[0] = inside(has_west, rows_of_left.T + west[:, 2 * basis : 3 * basis])
-    out_ref[2] = inside(has_east, rows_of_right.T + east[:, 2 * basis : 3 * basis])
+    out_ref[0] = inside(has_west, out_ref[0] + west[:, 2 * basis : 3 * basis])
+    out_ref[2] = inside(has_east, out_ref[2] + east[:, 2 * basis : 3 * basis])
     out_ref[3] = inside(has_below & has_west, -(below[:, :basis] + west[:, basis : 2 * basis]))
-    out_ref[4] = inside(has_below, -(below[:, basis : 2 * basis] + across_down))
+    out_ref[4] = inside(has_below, -(below[:, basis : 2 * basis] + out_ref[4]))
     out_ref[5] = inside(has_below & has_east, -(below[:, 2 * basis : 3 * basis] + east[:, basis : 2 * basis]))
     out_ref[6] = inside(has_above & has_west, -(above[:, :basis] + west[:, :basis]))
-    out_ref[7] = inside(has_above, -(above[:, basis : 2 * basis] + across_up))
+    out_ref[7] = inside(has_above, -(above[:, basis : 2 * basis] + out_ref[7]))
     out_ref[8] = inside(has_above & has_east, -(above[:, 2 * basis : 3 * basis] + east[:, :basis]))
-
-    for copy in [
-        strip_r, strip_l, edge_r, own_up, own_down, margin_up, margin_down, part_up, part_down, part_l, part_r,
-        *bulk_r, *bulk_l,
-    ]:
+    for copy in parts:
         copy.wait_send()
 
 
@@ -372,11 +411,15 @@
         pltpu.VMEM((2, margin + 1, layers, north), bf16),
         pltpu.VMEM((2, margin + 1, layers, north), bf16),
         pltpu.VMEM((4, margin, layers, north), f32),
+        pltpu.VMEM((2 * basis, rows), bf16),
+        pltpu.VMEM((3, rows, rows), bf16),
+        pltpu.VMEM((2, rows, rows), f32),
+        pltpu.VMEM((rows, basis), bf16),
         pltpu.VMEM((rows, planes * north), bf16),
         pltpu.VMEM((rows, cells * north), bf16),
         pltpu.VMEM((rows, cells * north), bf16),
         pltpu.VMEM((2, rows, margin * north), bf16),
-        pltpu.VMEM((rows, north), bf16),
+        pltpu.VMEM((basis, 1, layers, north), bf16),
         pltpu.VMEM((2, basis, margin, layers, north), bf16),
         pltpu.VMEM((2, rows, margin * north), bf16),
         pltpu.VMEM((2 * basis, planes * north), bf16),

time: 30.3 us -> 27.4 us (0.904)
  Pallas kernels: 29.6 us -> 26.6 us
    pallas_call x1, Pallas kernels: 28 us -> 25 us  [body(): pl.pallas_call(functools.partial(kernel, lat_n, depth_n), out_shape=jax.S...]
where the time goes in v3:
time: 27.4 us; the launch traced here: 27.3 us
  Pallas kernels  26.6 us (97%)
  between operations  0.64 us (2%)
    pallas_call x1, Pallas kernels, body(): pl.pallas_call(functools.partial(kernel, lat_n, depth_n), out_shape=jax.S...  25 us
    pallas_call x1, Pallas kernels, body(): pl.pallas_call(hand_out, out_shape=(jax.ShapeDtypeStruct((1, 1, 3, basis,...  1.59 us

profile of v3, /device:TPU:70, one launch (start us, length us, event | category | flops | bytes accessed | tf_op | source)
XLA Modules:
  0.0 27.3 jit_solution(6131543324038531003)
XLA Ops:
  0.6 25.0 %shard_map.77.blocks_ref = f32[9,32,32]{2,1,0:T(8,128)} custom-call(bf16[32,40,8,128]{3,2,1,0:T(8,128)(2,1)} %own_hbm.1, bf16[32,16,8,128]{3,2,1,0:T(8,128)(2,1)} %left_hbm.1, bf16[32,16,8,128]{3,2,1,0:T(8,128)(2,1)} %right_hbm.1, f32[40,8,128]{2,1,0:T(8,128)} %perm_hbm.1, s32[8,40]{1,0:T(8,128)} %bitcast.1, s32[1,1,2]{2,1,0:T(1,128)} %width_hbm.1), custom_call_target="tpu_custom_call" | custom-call | tf_op jit(solution)/shard_map/pallas_call | solution.py:434
  25.7 1.6 %shard_map.78 = (f32[1,1,3,32,32]{4,3,2,1,0:T(8,128)}, f32[1,1,2,3,32,32]{5,4,3,2,1,0:T(8,128)}) custom-call(f32[9,32,32]{2,1,0:T(8,128)} %shard_map.77.blocks_ref), custom_call_target="tpu_custom_call" | custom-call | tf_op jit(solution)/shard_map/pallas_call | solution.py:444

commit v4 on v3

--- a/solution.py
+++ b/solution.py
@@ -171,7 +171,7 @@
         bulk_l.append(remote(BULK_L + c, left_hbm.at[:, part], land_v.at[1, :, part], "left"))
         bulk_r[c].start()
         bulk_l[c].start()
-        if c == 0:
+        if c == 1:
             edge_r = remote(EDGE_R, own_hbm.at[:, pl.ds(cells - 1, 1)], edge_in, "right")
             edge_r.start()
         begins.append(begin)
@@ -433,7 +433,7 @@
     ]
     blocks = pl.pallas_call(
         functools.partial(kernel, lat_n, depth_n),
-        out_shape=jax.ShapeDtypeStruct((9, basis, basis), f32),
+        out_shape=pltpu.VMEM((9, basis, basis), f32),
         in_specs=[any_space] * 6,
         out_specs=vmem,
         scratch_shapes=scratch,

time: 27.4 us -> 27.4 us (level)
  local copies, waits for them, and re-layouts: 0 us -> 0.64 us
  Pallas kernels: 26.6 us -> 26 us
    pallas_call x1, Pallas kernels: 25 us -> 24.4 us  [body(): pl.pallas_call(functools.partial(kernel, lat_n, depth_n), out_shape=pltpu...]
    unnamed x0 -> x2, local copies, waits for them, and re-layouts: none -> 0.64 us
where the time goes in v4:
time: 27.4 us; the launch traced here: 27.3 us
  Pallas kernels  26 us (95%)
  between operations  0.65 us (2%)
  local copies, waits for them, and re-layouts  0.64 us (2%)
    pallas_call x1, Pallas kernels, body(): pl.pallas_call(functools.partial(kernel, lat_n, depth_n), out_shape=pltpu...  24.4 us
    pallas_call x1, Pallas kernels, body(): pl.pallas_call(hand_out, out_shape=(jax.ShapeDtypeStruct((1, 1, 3, basis,...  1.59 us
    unnamed x2, local copies, waits for them, and re-layouts  0.64 us

profile of v4, /device:TPU:70, one launch (start us, length us, event | category | flops | bytes accessed | tf_op | source)
XLA Modules:
  0.0 27.3 jit_solution(11461790787051851842)
XLA Ops:
  0.6 24.4 %shard_map.77.blocks_ref = f32[9,32,32]{2,1,0:T(8,128)S(1)} custom-call(bf16[32,40,8,128]{3,2,1,0:T(8,128)(2,1)} %own_hbm.1, bf16[32,16,8,128]{3,2,1,0:T(8,128)(2,1)} %left_hbm.1, bf16[32,16,8,128]{3,2,1,0:T(8,128)(2,1)} %right_hbm.1, f32[40,8,128]{2,1,0:T(8,128)} %perm_hbm.1, s32[8,40]{1,0:T(8,128)} %bitcast.1, s32[1,1,2]{2,1,0:T(1,128)} %width_hbm.1), custom_call_target="tpu_custom_call" | custom-call | tf_op jit(solution)/shard_map/pallas_call | solution.py:434
  25.0 0.0 copy-start
  25.0 0.6 %copy-done = f32[9,32,32]{2,1,0:T(8,128)} copy-done((f32[9,32,32]{2,1,0:T(8,128)}, f32[9,32,32]{2,1,0:T(8,128)S(1)}, u32[]{:S(2)}) %copy-start) | copy-done | bytes 36888
  25.7 1.6 %shard_map.78 = (f32[1,1,3,32,32]{4,3,2,1,0:T(8,128)}, f32[1,1,2,3,32,32]{5,4,3,2,1,0:T(8,128)}) custom-call(f32[9,32,32]{2,1,0:T(8,128)} %copy-done), custom_call_target="tpu_custom_call" | custom-call | tf_op jit(solution)/shard_map/pallas_call | solution.py:444
Async XLA Ops:
  25.0 0.7 %copy-start = (f32[9,32,32]{2,1,0:T(8,128)}, f32[9,32,32]{2,1,0:T(8,128)S(1)}, u32[]{:S(2)}) copy-start(f32[9,32,32]{2,1,0:T(8,128)S(1)} %shard_map.77.blocks_ref) | copy-start | bytes 110596
